TPU v7x, 256 devices: a whole 4x4x8 slice. The times are simulated.
256 devices in a mesh: gx: 16 (over y, z_lo, core), gy: 4 (over z_hi), gz: 4 (over x).
Axes of the slice: x: 4, y: 4, z: 8 (z_hi: 4, z_lo: 2; z = z_hi * 2 + z_lo), core: 2. Of those that a mesh axis runs over, the one named last changes fastest.
Arguments:
- positions: float32 [3, 65536], P(None, ('gx', 'gy', 'gz')), may hold values from 0 to 1
- species: int32 [65536], P(('gx', 'gy', 'gz')), may hold values from 0 to 3
- neighbors: int32 [64, 65536], P(None, ('gx', 'gy', 'gz')), may hold values from 0 to 768, as said below
- atom_count: int32 [256], P(('gx', 'gy', 'gz')), may hold values from 32 to 256, as said below
- ghost_x: int32 [256, 2, 128], P(('gx', 'gy', 'gz')), may hold values from 0 to 255, as said below
- ghost_yz: int32 [256, 4, 64], P(('gx', 'gy', 'gz')), may hold values from 0 to 255, as said below
- embedding: bfloat16 [4, 512], replicated, may hold values from -6 to 6
- filters: bfloat16 [2, 8, 512], replicated, may hold values from -2 to 2
- update_u: bfloat16 [2, 4, 128, 128], replicated, may hold values from -0.5 to 0.5
- update_v: bfloat16 [2, 4, 128, 128], replicated, may hold values from -0.5 to 0.5
- force_w: bfloat16 [4, 128, 8], replicated, may hold values from -0.5 to 0.5
Outputs:
- force_mean: float32 [3, 65536], P(None, ('gx', 'gy', 'gz'))
- deviation: float32 [65536], P(('gx', 'gy', 'gz'))
Inputs may be any that keep to these rules, and one draw needn't show every extreme that they name: `atom_count`: each domain holds 256 // 2**k live atoms for some k of 0 to 3; at least one domain holds exactly 256. `ghost_x`: indices of live atoms of the lending domain (below its atom_count); entry 0 of face 0 is its last live atom. `ghost_yz`: indices of live atoms of the lending domain (below its atom_count). `neighbors`: for a live atom, slots 0 to 31 hold a live own atom or the empty mark 256 + 8 * 64; the other slots hold the empty mark or a ghost row of a face that the atom lies near: ten times its coordinate along that face's axis is below 2 for a lower face, 8 or more for an upper one. A dead atom's slots are all empty. Slot 0 of each domain's first atom is 0.
All inputs are finite; a program needn't handle non-finite values.
Results may differ from a plain program's by a relative error of at most 0.02.
Values sent between devices are 32-bit elements; how exact they have to be, the bound alone decides.
A program may use at most 64 MiB of HBM per device.

v0:
```python
import jax
import jax.numpy as jnp
from jax import lax
from jax.sharding import PartitionSpec as P

MODELS = 4
KB = 8
LAYERS = 2


EDGE_LENGTH_SCALE = 0.125
SPACING = 0.5
SHARPNESS = 2.0
group_width = 8


def from_behind(x, axis, by):
    peers = lax.axis_size(axis)
    return lax.ppermute(x, axis, [(i, (i + by) % peers) for i in range(peers)])


def radial(squared, count_basis):
    centres = SPACING * jnp.arange(count_basis, dtype=jnp.float32)
    return jnp.exp(
        -jnp.square(
            (squared[None] - centres.reshape((count_basis,) + (1,) * squared.ndim)) * SHARPNESS
        )
    )


def face_pieces(source, along, ghost_x, ghost_yz):
    pieces = []
    for face_no, offset in ((0, 1), (1, -1)):
        chosen = jnp.take(source, ghost_x[0, face_no], axis=along)
        pieces.append(from_behind(chosen, "gx", offset))
    for face_no, offset in ((0, 1), (1, -1)):
        chosen = jnp.take(source, ghost_yz[0, face_no], axis=along)
        pieces.append(from_behind(chosen, "gy", offset))
    for face_no, offset in ((2, 1), (3, -1)):
        chosen = jnp.take(source, ghost_yz[0, face_no], axis=along)
        pieces.append(from_behind(chosen, "gz", offset))
    return pieces


def exchange_features(own_feat, ghost_x, ghost_yz):
    width_c = own_feat.shape[1] // MODELS
    columns = []
    for model_no in range(MODELS):
        pieces = face_pieces(
            own_feat[:, model_no * width_c : (model_no + 1) * width_c], 0, ghost_x, ghost_yz
        )
        columns.append(jnp.concatenate(pieces, axis=0))
    return jnp.concatenate(columns, axis=1)


def embed_rows(species_vals, embedding):
    one_hot = (
        species_vals[:, None] == jnp.arange(embedding.shape[0], dtype=jnp.float32)[None, :]
    ).astype(jnp.bfloat16)
    return jnp.dot(one_hot, embedding, preferred_element_type=jnp.float32)


def message(slot_ids, radial_blk, feat_table, filter_w):
    rows_n = slot_ids.shape[1]
    summed = jnp.zeros((rows_n, feat_table.shape[1]), jnp.float32)
    for first_slot in range(0, slot_ids.shape[0], group_width):
        group_ids = slot_ids[first_slot : first_slot + group_width]
        radial_g = radial_blk[:, first_slot : first_slot + group_width]
        weights = jnp.einsum("ksr,kc->src", radial_g, filter_w)
        summed = summed + jnp.sum(weights * feat_table[group_ids], axis=0)
    return EDGE_LENGTH_SCALE * summed


def refresh(summed_messages, current, mat_u, mat_v):
    rows_n = current.shape[0]
    models = mat_u.shape[0]
    width_c = mat_u.shape[1]
    summed_q = summed_messages.astype(jnp.bfloat16).reshape(rows_n, models, width_c)
    current_q = current.astype(jnp.bfloat16).reshape(rows_n, models, width_c)
    pre_act = jnp.einsum("rmc,mce->rme", summed_q, mat_u, preferred_element_type=jnp.float32)
    pre_act = pre_act + jnp.einsum(
        "rmc,mce->rme", current_q, mat_v, preferred_element_type=jnp.float32
    )
    return current + jax.nn.silu(pre_act).reshape(rows_n, models * width_c)


def local(
    positions,
    species,
    neighbors,
    atom_count,
    ghost_x,
    ghost_yz,
    embedding,
    filters,
    update_u,
    update_v,
    force_w,
):
    atoms_n = positions.shape[1]
    ghosts_n = 2 * ghost_x.shape[2] + 4 * ghost_yz.shape[2]
    empty_mark = atoms_n + ghosts_n
    block_n = min(128, atoms_n)
    live_n = atom_count[0]
    blocks_live = (live_n + block_n - 1) // block_n
    species_f = species.astype(jnp.float32)
    packed = jnp.concatenate([positions, species_f[None]], axis=0)
    received = face_pieces(packed, 1, ghost_x, ghost_yz)
    shifted = []
    for number, arrived in enumerate(received):
        axis_no = number // 2
        direction = 2.0 * (number % 2) - 1.0
        shifted.append(
            arrived + direction * (jnp.arange(4) == axis_no).astype(jnp.float32)[:, None]
        )
    ghost_pack = jnp.concatenate(shifted, axis=1)
    ghost_pos = ghost_pack[:3]
    zero_col = jnp.zeros((3, 1), jnp.float32)
    pos_full = jnp.concatenate([positions, ghost_pos, zero_col], axis=1)
    present = (neighbors < empty_mark).astype(jnp.float32)
    displacement_all = pos_full[:, neighbors] - positions[:, None, :]
    radial_all = radial(jnp.sum(displacement_all * displacement_all, axis=0), KB) * present[None]
    own_feat = embed_rows(species_f, embedding)
    ghost_feat = embed_rows(ghost_pack[3], embedding)
    zero_row = jnp.zeros((1, own_feat.shape[1]), jnp.float32)
    for layer_no in range(LAYERS):
        filter_w = filters[layer_no].astype(jnp.float32)
        mat_u = update_u[layer_no]
        mat_v = update_v[layer_no]
        if layer_no > 0:
            ghost_feat = exchange_features(own_feat, ghost_x, ghost_yz)
        feat_full = jnp.concatenate([own_feat, ghost_feat, zero_row], axis=0)

        def whole_block(block_no, result):
            first_row = block_no * block_n
            slot_ids = lax.dynamic_slice_in_dim(neighbors, first_row, block_n, 1)
            radial_blk = lax.dynamic_slice_in_dim(radial_all, first_row, block_n, 2)
            current = lax.dynamic_slice_in_dim(own_feat, first_row, block_n, 0)
            summed_messages = message(slot_ids, radial_blk, feat_full, filter_w)
            return lax.dynamic_update_slice_in_dim(
                result, refresh(summed_messages, current, mat_u, mat_v), first_row, 0
            )

        own_next = lax.fori_loop(0, blocks_live, whole_block, jnp.zeros_like(own_feat))
        own_feat = own_next

    def force_section(block_no, outputs):
        mean_all, spread = outputs
        first_row = block_no * block_n
        current = lax.dynamic_slice_in_dim(own_feat, first_row, block_n, 0)
        current_q = current.astype(jnp.bfloat16).reshape(
            block_n, force_w.shape[0], force_w.shape[1]
        )
        basis_coefficients = jnp.einsum(
            "rmc,mck->mkr", current_q, force_w, preferred_element_type=jnp.float32
        )
        displacement_vectors = lax.dynamic_slice_in_dim(displacement_all, first_row, block_n, 2)
        radial_terms = lax.dynamic_slice_in_dim(radial_all, first_row, block_n, 2)
        coupling_strength = jnp.einsum("jdp,hjp->hdp", radial_terms, basis_coefficients)
        atomic_forces = EDGE_LENGTH_SCALE * jnp.einsum(
            "wue,hue->whe", coupling_strength, displacement_vectors
        )
        average = jnp.mean(atomic_forces, axis=0)
        spread_blk = jnp.mean(jnp.sum(jnp.square(atomic_forces - average[None]), axis=1), axis=0)
        alive_rows = (first_row + jnp.arange(block_n) < live_n).astype(jnp.float32)
        mean_all = lax.dynamic_update_slice_in_dim(
            mean_all, average * alive_rows[None, :], first_row, 1
        )
        spread = lax.dynamic_update_slice_in_dim(spread, spread_blk * alive_rows, first_row, 0)
        return (mean_all, spread)

    empty_out = (jnp.zeros((3, atoms_n), jnp.float32), jnp.zeros((atoms_n,), jnp.float32))
    force_mean, deviation = lax.fori_loop(0, blocks_live, force_section, empty_out)
    return (force_mean, deviation)


def solution(mesh):
    in_specs = (
        P(None, ("gx", "gy", "gz")),
        P(("gx", "gy", "gz")),
        P(None, ("gx", "gy", "gz")),
        P(("gx", "gy", "gz")),
        P(("gx", "gy", "gz"), None, None),
        P(("gx", "gy", "gz"), None, None),
        P(),
        P(),
        P(),
        P(),
        P(),
    )
    out_specs = (P(None, ("gx", "gy", "gz")), P(("gx", "gy", "gz")))
    return jax.shard_map(local, mesh=mesh, in_specs=in_specs, out_specs=out_specs, check_vma=False)
```

profile of v0, /device:TPU:6, one launch (start us, length us, event | category | flops | bytes accessed | tf_op | source)
XLA Modules:
  0.0 440.2 jit_solution(6841482477024222310)
XLA Ops:
  8.5 6.4 %collective-permute-start.3 = (f32[4,64]{1,0:T(4,128)S(1)}, f32[4,64]{1,0:T(4,128)S(1)}, u32[]{:S(2)}, u32[]{:S(2)}) collective-permute-start(f32[4,64]{1,0:T(4,128)S(1)} %select_bitcast_fusion.2), channel_id=1, source_target_pairs={{0,12},{4,0},{8,4},{12,8},{1,13},{5,1},{9,5},{13,9},{2,14},{6,2},{... | collective-permute-start | bytes 3080 | tf_op jit(solution)/shard_map/ppermute | solution.py:19
  34.6 54.8 %gather_fusion.16 = f32[16384,3]{1,0:T(8,128)} fusion(f32[3,769]{0,1:T(8,128)S(1)} %copy.148, s32[16384]{0:T(1024)S(1)} %broadcast_clamp_fusion), kind=kCustom, calls=%fused_computation.46 | custom fusion | bytes 458752 | tf_op jit(solution)/shard_map/gather | solution.py:121
  89.3 6.6 %copy.149 = f32[64,256,3]{0,2,1:T(4,128)S(1)} copy(f32[64,256,3]{2,1,0:T(8,128)} %bitcast.335) | data formatting | bytes 393216 | tf_op jit(solution)/shard_map/gather | solution.py:121
  101.0 122.8 %while.32 = (s32[]{:T(128)}, f32[256,512]{0,1:T(8,128)}, s32[]{:T(128)}, f32[256,512]{1,0:T(8,128)}, bf16[8,64,256]{2,0,1:T(8,128)(2,1)}, /*index=5*/bf16[8,512]...) while((s32[]{:T(128)}, f32[256,512]{0,1:T(8,128)}, ...), condition=%wide.region_10.13_spmd, body=%wide.region_1.12_spmd.sunk | while | flops 109608976 | bytes 65438196 | solution.py:144
  101.2 4.9 %gather_fusion = f32[1024,512]{1,0:T(8,128)} fusion(f32[769,512]{1,0:T(8,128)S(1)} %get-tuple-element.707, s32[1024]{0:T(1024)S(1)} %get-tuple-element.619), kind=kCustom, calls=%fused_computation.9.clone.1 | custom fusion | bytes 4198400 | tf_op jit(solution)/shard_map/while/body/gather | solution.py:70
  108.2 4.9 %gather_fusion.1 = f32[1024,512]{1,0:T(8,128)} fusion(f32[769,512]{1,0:T(8,128)S(1)} %get-tuple-element.707, s32[1024]{0:T(1024)S(1)} %get-tuple-element.620), kind=kCustom, calls=%fused_computation.8.clone.1 | custom fusion | bytes 4198400 | tf_op jit(solution)/shard_map/while/body/gather | solution.py:70
  115.2 4.9 %gather_fusion.2 = f32[1024,512]{1,0:T(8,128)} fusion(f32[769,512]{1,0:T(8,128)S(1)} %get-tuple-element.707, s32[1024]{0:T(1024)S(1)} %get-tuple-element.621), kind=kCustom, calls=%fused_computation.7.clone.1 | custom fusion | bytes 4198400 | tf_op jit(solution)/shard_map/while/body/gather | solution.py:70
  122.2 4.9 %gather_fusion.3 = f32[1024,512]{1,0:T(8,128)} fusion(f32[769,512]{1,0:T(8,128)S(1)} %get-tuple-element.707, s32[1024]{0:T(1024)S(1)} %get-tuple-element.622), kind=kCustom, calls=%fused_computation.6.clone.1 | custom fusion | bytes 4198400 | tf_op jit(solution)/shard_map/while/body/gather | solution.py:70
  129.2 4.9 %gather_fusion.4 = f32[1024,512]{1,0:T(8,128)} fusion(f32[769,512]{1,0:T(8,128)S(1)} %get-tuple-element.707, s32[1024]{0:T(1024)S(1)} %get-tuple-element.623), kind=kCustom, calls=%fused_computation.5.clone.1 | custom fusion | bytes 4198400 | tf_op jit(solution)/shard_map/while/body/gather | solution.py:70
  136.3 4.9 %gather_fusion.5 = f32[1024,512]{1,0:T(8,128)} fusion(f32[769,512]{1,0:T(8,128)S(1)} %get-tuple-element.707, s32[1024]{0:T(1024)S(1)} %get-tuple-element.624), kind=kCustom, calls=%fused_computation.4.clone.1 | custom fusion | bytes 4198400 | tf_op jit(solution)/shard_map/while/body/gather | solution.py:70
  143.3 4.9 %gather_fusion.6 = f32[1024,512]{1,0:T(8,128)} fusion(f32[769,512]{1,0:T(8,128)S(1)} %get-tuple-element.707, s32[1024]{0:T(1024)S(1)} %get-tuple-element.625), kind=kCustom, calls=%fused_computation.2.clone.1 | custom fusion | bytes 4198400 | tf_op jit(solution)/shard_map/while/body/gather | solution.py:70
  150.3 4.9 %gather_fusion.7 = f32[1024,512]{1,0:T(8,128)} fusion(f32[769,512]{1,0:T(8,128)S(1)} %get-tuple-element.707, s32[1024]{0:T(1024)S(1)} %get-tuple-element.626), kind=kCustom, calls=%fused_computation.3.clone.1 | custom fusion | bytes 4198400 | tf_op jit(solution)/shard_map/while/body/gather | solution.py:70
  162.5 4.9 %gather_fusion = f32[1024,512]{1,0:T(8,128)} fusion(f32[769,512]{1,0:T(8,128)S(1)} %get-tuple-element.707, s32[1024]{0:T(1024)S(1)} %get-tuple-element.619), kind=kCustom, calls=%fused_computation.9.clone.1 | custom fusion | bytes 4198400 | tf_op jit(solution)/shard_map/while/body/gather | solution.py:70
  176.5 4.9 %gather_fusion.2 = f32[1024,512]{1,0:T(8,128)} fusion(f32[769,512]{1,0:T(8,128)S(1)} %get-tuple-element.707, s32[1024]{0:T(1024)S(1)} %get-tuple-element.621), kind=kCustom, calls=%fused_computation.7.clone.1 | custom fusion | bytes 4198400 | tf_op jit(solution)/shard_map/while/body/gather | solution.py:70
  183.5 4.9 %gather_fusion.3 = f32[1024,512]{1,0:T(8,128)} fusion(f32[769,512]{1,0:T(8,128)S(1)} %get-tuple-element.707, s32[1024]{0:T(1024)S(1)} %get-tuple-element.622), kind=kCustom, calls=%fused_computation.6.clone.1 | custom fusion | bytes 4198400 | tf_op jit(solution)/shard_map/while/body/gather | solution.py:70
  190.6 4.9 %gather_fusion.4 = f32[1024,512]{1,0:T(8,128)} fusion(f32[769,512]{1,0:T(8,128)S(1)} %get-tuple-element.707, s32[1024]{0:T(1024)S(1)} %get-tuple-element.623), kind=kCustom, calls=%fused_computation.5.clone.1 | custom fusion | bytes 4198400 | tf_op jit(solution)/shard_map/while/body/gather | solution.py:70
  197.6 4.9 %gather_fusion.5 = f32[1024,512]{1,0:T(8,128)} fusion(f32[769,512]{1,0:T(8,128)S(1)} %get-tuple-element.707, s32[1024]{0:T(1024)S(1)} %get-tuple-element.624), kind=kCustom, calls=%fused_computation.4.clone.1 | custom fusion | bytes 4198400 | tf_op jit(solution)/shard_map/while/body/gather | solution.py:70
  204.6 4.9 %gather_fusion.6 = f32[1024,512]{1,0:T(8,128)} fusion(f32[769,512]{1,0:T(8,128)S(1)} %get-tuple-element.707, s32[1024]{0:T(1024)S(1)} %get-tuple-element.625), kind=kCustom, calls=%fused_computation.2.clone.1 | custom fusion | bytes 4198400 | tf_op jit(solution)/shard_map/while/body/gather | solution.py:70
  246.6 5.8 %collective-permute-done.12 = f32[128,128]{1,0:T(8,128)S(1)} collective-permute-done((f32[128,128]{1,0:T(8,128)S(1)}, f32[128,128]{1,0:T(8,128)S(1)}, u32[]{:S(2)}, u32[]{:S(2)}) %collective-permute-start.12) | collective-permute-done | bytes 65568 | tf_op jit(solution)/shard_map/ppermute | solution.py:19
  252.4 5.8 %collective-permute-done.18 = f32[128,128]{1,0:T(8,128)S(1)} collective-permute-done((f32[128,128]{1,0:T(8,128)S(1)}, f32[128,128]{1,0:T(8,128)S(1)}, u32[]{:S(2)}, u32[]{:S(2)}) %collective-permute-start.18) | collective-permute-done | bytes 65568 | tf_op jit(solution)/shard_map/ppermute | solution.py:19
  258.2 5.8 %collective-permute-done.24 = f32[128,128]{1,0:T(8,128)S(1)} collective-permute-done((f32[128,128]{1,0:T(8,128)S(1)}, f32[128,128]{1,0:T(8,128)S(1)}, u32[]{:S(2)}, u32[]{:S(2)}) %collective-permute-start.24) | collective-permute-done | bytes 65568 | tf_op jit(solution)/shard_map/ppermute | solution.py:19
  302.6 124.0 %while.33 = (s32[]{:T(128)}, bf16[256,512]{0,1:T(8,128)(2,1)}, s32[]{:T(128)}, f32[256,512]{0,1:T(8,128)}, bf16[8,64,256]{2,0,1:T(8,128)(2,1)}, /*index=5*/bf16[...) while((s32[]{:T(128)}, bf16[256,512]{0,1:T(8,128)(2,1)}, ...), condition=%wide.region_20.25_spmd, body=%wide.region_11.24_spmd.sunk | while | flops 109608976 | bytes 63603188 | solution.py:144
  302.7 4.9 %gather_fusion.9 = f32[1024,512]{1,0:T(8,128)} fusion(f32[769,512]{1,0:T(8,128)S(1)} %get-tuple-element.770, s32[1024]{0:T(1024)S(1)} %get-tuple-element.638), kind=kCustom, calls=%fused_computation.18.clone.1 | custom fusion | bytes 4198400 | tf_op jit(solution)/shard_map/while/body/gather | solution.py:70
  426.7 12.4 %while.34 = (s32[]{:T(128)}, f32[3,256]{1,0:T(4,128)S(1)}, f32[256]{0:T(256)S(1)}, s32[]{:T(128)}, bf16[3,64,256]{1,0,2:T(4,128)(2,1)}, /*index=5*/bf16[256,512]...) while((s32[]{:T(128)}, f32[3,256]{1,0:T(4,128)S(1)}, ...), condition=%wide.region_24.29_spmd, body=%wide.region_21.28_spmd.sunk | while | flops 1778310 | bytes 858311 | solution.py:173
  (390 shorter events, 278.5 us)
Async XLA Ops:
  3.8 25.2 %collective-permute-start.5 = (f32[4,64]{1,0:T(4,128)S(1)}, f32[4,64]{1,0:T(4,128)S(1)}, u32[]{:S(2)}, u32[]{:S(2)}) collective-permute-start(f32[4,64]{1,0:T(4,128)S(1)} %select_bitcast_fusion), channel_id=1, source_target_pairs={{0,3},{1,0},{2,1},{3,2},{4,7},{5,4},{6,5},{7,6},{8,11},{9,8},{10,9... | collective-permute-start | bytes 3080 | tf_op jit(solution)/shard_map/ppermute | solution.py:19
  5.3 23.8 %collective-permute-start.4 = (f32[4,64]{1,0:T(4,128)S(1)}, f32[4,64]{1,0:T(4,128)S(1)}, u32[]{:S(2)}, u32[]{:S(2)}) collective-permute-start(f32[4,64]{1,0:T(4,128)S(1)} %select_bitcast_fusion.1), channel_id=1, source_target_pairs={{0,1},{1,2},{2,3},{3,0},{4,5},{5,6},{6,7},{7,4},{8,9},{9,10},{10,1... | collective-permute-start | bytes 3080 | tf_op jit(solution)/shard_map/ppermute | solution.py:19
  8.5 20.7 %collective-permute-start.3 = (f32[4,64]{1,0:T(4,128)S(1)}, f32[4,64]{1,0:T(4,128)S(1)}, u32[]{:S(2)}, u32[]{:S(2)}) collective-permute-start(f32[4,64]{1,0:T(4,128)S(1)} %select_bitcast_fusion.2), channel_id=1, source_target_pairs={{0,12},{4,0},{8,4},{12,8},{1,13},{5,1},{9,5},{13,9},{2,14},{6,2},{... | collective-permute-start | bytes 3080 | tf_op jit(solution)/shard_map/ppermute | solution.py:19
  15.5 13.8 %collective-permute-start.2 = (f32[4,64]{1,0:T(4,128)S(1)}, f32[4,64]{1,0:T(4,128)S(1)}, u32[]{:S(2)}, u32[]{:S(2)}) collective-permute-start(f32[4,64]{1,0:T(4,128)S(1)} %select_bitcast_fusion.3), channel_id=1, source_target_pairs={{0,4},{4,8},{8,12},{12,0},{1,5},{5,9},{9,13},{13,1},{2,6},{6,10},{... | collective-permute-start | bytes 3080 | tf_op jit(solution)/shard_map/ppermute | solution.py:19
  17.1 12.2 %collective-permute-start.1 = (f32[4,128]{1,0:T(4,128)S(1)}, f32[4,128]{1,0:T(4,128)S(1)}, u32[]{:S(2)}, u32[]{:S(2)}) collective-permute-start(f32[4,128]{1,0:T(4,128)S(1)} %select_bitcast_fusion.4), channel_id=1, source_target_pairs={{0,240},{16,0},{32,16},{48,32},{64,48},{80,64},{96,80},{112,96},{1... | collective-permute-start | bytes 6152 | tf_op jit(solution)/shard_map/ppermute | solution.py:19
  240.0 25.2 %collective-permute-start.7 = (f32[128,128]{1,0:T(8,128)S(1)}, f32[128,128]{1,0:T(8,128)S(1)}, u32[]{:S(2)}, u32[]{:S(2)}) collective-permute-start(f32[128,128]{1,0:T(8,128)S(1)} %get-tuple-element.428), channel_id=1, source_target_pairs={{0,240},{16,0},{32,16},{48,32},{64,48},{80,64},{96,80},{112,96},{1... | collective-permute-start | bytes 196616 | tf_op jit(solution)/shard_map/ppermute | solution.py:19
  240.2 6.1 %collective-permute-start.6 = (f32[128,128]{1,0:T(8,128)S(1)}, f32[128,128]{1,0:T(8,128)S(1)}, u32[]{:S(2)}, u32[]{:S(2)}) collective-permute-start(f32[128,128]{1,0:T(8,128)S(1)} %get-tuple-element.432), channel_id=1, source_target_pairs={{0,16},{16,32},{32,48},{48,64},{64,80},{80,96},{96,112},{112,128},... | collective-permute-start | bytes 196616 | tf_op jit(solution)/shard_map/ppermute | solution.py:19
  240.9 38.0 %collective-permute-start.8 = (f32[64,128]{1,0:T(8,128)S(1)}, f32[64,128]{1,0:T(8,128)S(1)}, u32[]{:S(2)}, u32[]{:S(2)}) collective-permute-start(f32[64,128]{1,0:T(8,128)S(1)} %get-tuple-element.424), channel_id=1, source_target_pairs={{0,4},{4,8},{8,12},{12,0},{1,5},{5,9},{9,13},{13,1},{2,6},{6,10},{... | collective-permute-start | bytes 98312 | tf_op jit(solution)/shard_map/ppermute | solution.py:19
  241.1 42.0 %collective-permute-start.9 = (f32[64,128]{1,0:T(8,128)S(1)}, f32[64,128]{1,0:T(8,128)S(1)}, u32[]{:S(2)}, u32[]{:S(2)}) collective-permute-start(f32[64,128]{1,0:T(8,128)S(1)} %get-tuple-element.420), channel_id=1, source_target_pairs={{0,12},{4,0},{8,4},{12,8},{1,13},{5,1},{9,5},{13,9},{2,14},{6,2},{... | collective-permute-start | bytes 98312 | tf_op jit(solution)/shard_map/ppermute | solution.py:19
  245.4 39.8 %collective-permute-start.10 = (f32[64,128]{1,0:T(8,128)S(1)}, f32[64,128]{1,0:T(8,128)S(1)}, u32[]{:S(2)}, u32[]{:S(2)}) collective-permute-start(f32[64,128]{1,0:T(8,128)S(1)} %get-tuple-element.416), channel_id=1, source_target_pairs={{0,1},{1,2},{2,3},{3,0},{4,5},{5,6},{6,7},{7,4},{8,9},{9,10},{10,1... | collective-permute-start | bytes 98312 | tf_op jit(solution)/shard_map/ppermute | solution.py:19
  246.3 6.0 %collective-permute-start.12 = (f32[128,128]{1,0:T(8,128)S(1)}, f32[128,128]{1,0:T(8,128)S(1)}, u32[]{:S(2)}, u32[]{:S(2)}) collective-permute-start(f32[128,128]{1,0:T(8,128)S(1)} %get-tuple-element.433), channel_id=1, source_target_pairs={{0,16},{16,32},{32,48},{48,64},{64,80},{80,96},{96,112},{112,128},... | collective-permute-start | bytes 196616 | tf_op jit(solution)/shard_map/ppermute | solution.py:19
  263.9 21.3 %collective-permute-start.11 = (f32[64,128]{1,0:T(8,128)S(1)}, f32[64,128]{1,0:T(8,128)S(1)}, u32[]{:S(2)}, u32[]{:S(2)}) collective-permute-start(f32[64,128]{1,0:T(8,128)S(1)} %get-tuple-element.412), channel_id=1, source_target_pairs={{0,3},{1,0},{2,1},{3,2},{4,7},{5,4},{6,5},{7,6},{8,11},{9,8},{10,9... | collective-permute-start | bytes 98312 | tf_op jit(solution)/shard_map/ppermute | solution.py:19
  278.9 6.4 %collective-permute-start.14 = (f32[64,128]{1,0:T(8,128)S(1)}, f32[64,128]{1,0:T(8,128)S(1)}, u32[]{:S(2)}, u32[]{:S(2)}) collective-permute-start(f32[64,128]{1,0:T(8,128)S(1)} %get-tuple-element.425), channel_id=1, source_target_pairs={{0,4},{4,8},{8,12},{12,0},{1,5},{5,9},{9,13},{13,1},{2,6},{6,10},{... | collective-permute-start | bytes 98312 | tf_op jit(solution)/shard_map/ppermute | solution.py:19
  278.9 10.5 %collective-permute-start.15 = (f32[64,128]{1,0:T(8,128)S(1)}, f32[64,128]{1,0:T(8,128)S(1)}, u32[]{:S(2)}, u32[]{:S(2)}) collective-permute-start(f32[64,128]{1,0:T(8,128)S(1)} %get-tuple-element.421), channel_id=1, source_target_pairs={{0,12},{4,0},{8,4},{12,8},{1,13},{5,1},{9,5},{13,9},{2,14},{6,2},{... | collective-permute-start | bytes 98312 | tf_op jit(solution)/shard_map/ppermute | solution.py:19
  283.1 9.4 %collective-permute-start.16 = (f32[64,128]{1,0:T(8,128)S(1)}, f32[64,128]{1,0:T(8,128)S(1)}, u32[]{:S(2)}, u32[]{:S(2)}) collective-permute-start(f32[64,128]{1,0:T(8,128)S(1)} %get-tuple-element.417), channel_id=1, source_target_pairs={{0,1},{1,2},{2,3},{3,0},{4,5},{5,6},{6,7},{7,4},{8,9},{9,10},{10,1... | collective-permute-start | bytes 98312 | tf_op jit(solution)/shard_map/ppermute | solution.py:19
  285.1 7.4 %collective-permute-start.17 = (f32[64,128]{1,0:T(8,128)S(1)}, f32[64,128]{1,0:T(8,128)S(1)}, u32[]{:S(2)}, u32[]{:S(2)}) collective-permute-start(f32[64,128]{1,0:T(8,128)S(1)} %get-tuple-element.413), channel_id=1, source_target_pairs={{0,3},{1,0},{2,1},{3,2},{4,7},{5,4},{6,5},{7,6},{8,11},{9,8},{10,9... | collective-permute-start | bytes 98312 | tf_op jit(solution)/shard_map/ppermute | solution.py:19
  285.2 7.4 %collective-permute-start.20 = (f32[64,128]{1,0:T(8,128)S(1)}, f32[64,128]{1,0:T(8,128)S(1)}, u32[]{:S(2)}, u32[]{:S(2)}) collective-permute-start(f32[64,128]{1,0:T(8,128)S(1)} %get-tuple-element.426), channel_id=1, source_target_pairs={{0,4},{4,8},{8,12},{12,0},{1,5},{5,9},{9,13},{13,1},{2,6},{6,10},{... | collective-permute-start | bytes 98312 | tf_op jit(solution)/shard_map/ppermute | solution.py:19
  285.3 10.9 %collective-permute-start.21 = (f32[64,128]{1,0:T(8,128)S(1)}, f32[64,128]{1,0:T(8,128)S(1)}, u32[]{:S(2)}, u32[]{:S(2)}) collective-permute-start(f32[64,128]{1,0:T(8,128)S(1)} %get-tuple-element.422), channel_id=1, source_target_pairs={{0,12},{4,0},{8,4},{12,8},{1,13},{5,1},{9,5},{13,9},{2,14},{6,2},{... | collective-permute-start | bytes 98312 | tf_op jit(solution)/shard_map/ppermute | solution.py:19
  289.4 6.9 %collective-permute-start.22 = (f32[64,128]{1,0:T(8,128)S(1)}, f32[64,128]{1,0:T(8,128)S(1)}, u32[]{:S(2)}, u32[]{:S(2)}) collective-permute-start(f32[64,128]{1,0:T(8,128)S(1)} %get-tuple-element.418), channel_id=1, source_target_pairs={{0,1},{1,2},{2,3},{3,0},{4,5},{5,6},{6,7},{7,4},{8,9},{9,10},{10,1... | collective-permute-start | bytes 98312 | tf_op jit(solution)/shard_map/ppermute | solution.py:19
  292.5 6.6 %collective-permute-start.23 = (f32[64,128]{1,0:T(8,128)S(1)}, f32[64,128]{1,0:T(8,128)S(1)}, u32[]{:S(2)}, u32[]{:S(2)}) collective-permute-start(f32[64,128]{1,0:T(8,128)S(1)} %get-tuple-element.414), channel_id=1, source_target_pairs={{0,3},{1,0},{2,1},{3,2},{4,7},{5,4},{6,5},{7,6},{8,11},{9,8},{10,9... | collective-permute-start | bytes 98312 | tf_op jit(solution)/shard_map/ppermute | solution.py:19
  292.5 9.9 %collective-permute-start.29 = (f32[64,128]{1,0:T(8,128)S(1)}, f32[64,128]{1,0:T(8,128)S(1)}, u32[]{:S(2)}, u32[]{:S(2)}) collective-permute-start(f32[64,128]{1,0:T(8,128)S(1)} %get-tuple-element.415), channel_id=1, source_target_pairs={{0,3},{1,0},{2,1},{3,2},{4,7},{5,4},{6,5},{7,6},{8,11},{9,8},{10,9... | collective-permute-start | bytes 98312 | tf_op jit(solution)/shard_map/ppermute | solution.py:19
  292.7 9.7 %collective-permute-start.28 = (f32[64,128]{1,0:T(8,128)S(1)}, f32[64,128]{1,0:T(8,128)S(1)}, u32[]{:S(2)}, u32[]{:S(2)}) collective-permute-start(f32[64,128]{1,0:T(8,128)S(1)} %get-tuple-element.419), channel_id=1, source_target_pairs={{0,1},{1,2},{2,3},{3,0},{4,5},{5,6},{6,7},{7,4},{8,9},{9,10},{10,1... | collective-permute-start | bytes 98312 | tf_op jit(solution)/shard_map/ppermute | solution.py:19
  296.2 6.2 %collective-permute-start.27 = (f32[64,128]{1,0:T(8,128)S(1)}, f32[64,128]{1,0:T(8,128)S(1)}, u32[]{:S(2)}, u32[]{:S(2)}) collective-permute-start(f32[64,128]{1,0:T(8,128)S(1)} %get-tuple-element.423), channel_id=1, source_target_pairs={{0,12},{4,0},{8,4},{12,8},{1,13},{5,1},{9,5},{13,9},{2,14},{6,2},{... | collective-permute-start | bytes 98312 | tf_op jit(solution)/shard_map/ppermute | solution.py:19
  296.3 6.1 %collective-permute-start.26 = (f32[64,128]{1,0:T(8,128)S(1)}, f32[64,128]{1,0:T(8,128)S(1)}, u32[]{:S(2)}, u32[]{:S(2)}) collective-permute-start(f32[64,128]{1,0:T(8,128)S(1)} %get-tuple-element.427), channel_id=1, source_target_pairs={{0,4},{4,8},{8,12},{12,0},{1,5},{5,9},{9,13},{13,1},{2,6},{6,10},{... | collective-permute-start | bytes 98312 | tf_op jit(solution)/shard_map/ppermute | solution.py:19
  (59 other events, 667.3 us)
where the time goes:
time: 449 us; the launch traced here: 440 us
  local copies, waits for them, and re-layouts  259 us (58%)
  matrix products  79.4 us (18%)
  starting transfers between devices  46.6 us (10%)
  waiting for transfers between devices  31.6 us (7%)
  other arithmetic  19.7 us (4%)
    gather x32, local copies, waits for them, and re-layouts, message(): summed = summed + jnp.sum(weights * feat_table[group_ids], axis=0)  156 us
    dot_general x32, matrix products, message(): weights = jnp.einsum('ksr,kc->src', radial_g, filter_w)  67.6 us
    gather x2, local copies, waits for them, and re-layouts, local(): displacement_all = pos_full[:, neighbors] - positions[:, None, :]  61.3 us
    ppermute x30, starting transfers between devices, from_behind(): return lax.ppermute(x, axis, [(i, (i + by) % peers) for i in range(peers)])  46.6 us
    ppermute x30, waiting for transfers between devices, from_behind(): return lax.ppermute(x, axis, [(i, (i + by) % peers) for i in range(peers)])  31.6 us
    gather x24, local copies, waits for them, and re-layouts, face_pieces(): chosen = jnp.take(source, ghost_yz[0, face_no], axis=along)  12.2 us
  transfers between devices with their start and end apart: 30, of which 9 were waited for; matrix products, arithmetic and copies ran while one was open for 3% of the time, Pallas kernels for 0%

commit v1 on v0

v1 whole, which is shorter than its diff:
```python
import functools

import jax
import jax.numpy as jnp
from jax import lax
from jax.experimental import pallas as pl
from jax.experimental.pallas import tpu as pltpu
from jax.sharding import PartitionSpec as P

ATOMS_DEV = 256
GHOSTS = 512
TABLE = ATOMS_DEV + GHOSTS
MODELS = 4
C = 128
WIDTH = MODELS * C
KB = 8
SPECIES = 4
SLOTS_HALF = 32
SCALE = 0.125
ROOT_LOG2E = 1.2011224087864498
F32 = jnp.float32
BF16 = jnp.bfloat16
AXES = ("gx", "gy", "gz")


def iota(shape, dim):
    return lax.broadcasted_iota(jnp.int32, shape, dim)


def dot(a, b):
    return lax.dot_general(a, b, (((1,), (0,)), ((), ())), preferred_element_type=F32)


def split(x):
    high = x.astype(BF16).astype(F32)
    return high, (x - high).astype(BF16).astype(F32)


def add_silu(h, pre):
    half = 0.5 * pre
    return h + half + half * jnp.tanh(half)


def kernel(
    sizes,
    pos_ref, spec_ref, nbr_ref, live_ref, gx_ref, gyz_ref, emb_ref, filt_ref, u_hbm, v_hbm, fw_ref,
    mean_ref, dev_ref,
    sel, pack_send, pack_recv, agg_send, agg_recv, count, col, rad, left, feat, h_own, h_tab, acc,
    fbc, uvt, w_msg, w_emb, dsum, u_vm, v_vm,
    send_sem, recv_sem, copy_sem,
):
    here = [lax.axis_index(a) for a in AXES]
    peers = []
    for axis, size, me in zip(AXES, sizes, here):
        peers.append({axis: lax.rem(me + 1, size)})
        peers.append({axis: lax.rem(me + size - 1, size)})

    barrier = pltpu.get_barrier_semaphore()
    for peer in peers:
        pl.semaphore_signal(barrier, inc=1, device_id=peer, device_id_type=pl.DeviceIdType.MESH)
    u_copy = pltpu.make_async_copy(u_hbm, u_vm, copy_sem.at[0])
    v_copy = pltpu.make_async_copy(v_hbm, v_vm, copy_sem.at[1])
    u_copy.start()
    v_copy.start()

    lists = [gx_ref[0:1, :], gx_ref[1:2, :]]
    for pair in (0, 2):
        lists.append(jnp.concatenate([gyz_ref[pair : pair + 1, :], gyz_ref[pair + 1 : pair + 2, :]], axis=1))
    atom_row = iota((ATOMS_DEV, 128), 0)
    for g in range(4):
        sel[:, g * 128 : (g + 1) * 128] = jnp.where(atom_row == lists[g], 1.0, 0.0).astype(BF16)

    own = jnp.concatenate(
        [pos_ref[...], spec_ref[...].astype(F32), jnp.zeros((4, ATOMS_DEV), F32)], axis=0
    )
    high = own.astype(BF16).astype(F32)
    rest = own - high
    middle = rest.astype(BF16).astype(F32)
    low = rest - middle
    picked = dot(jnp.concatenate([high, middle, low], axis=0).astype(BF16), sel[...])
    picked = picked[0:8] + picked[8:16] + picked[16:24]
    for g in range(4):
        pack_send[g] = picked[:, g * 128 : (g + 1) * 128]

    def sends(source, target, first):
        return [
            pltpu.make_async_remote_copy(
                src_ref=source.at[group],
                dst_ref=target.at[face],
                send_sem=send_sem.at[first + face],
                recv_sem=recv_sem.at[first + face],
                device_id=peers[face],
                device_id_type=pl.DeviceIdType.MESH,
            )
            for face, group in enumerate((0, 1, 2, 2, 3, 3))
        ]

    pl.semaphore_wait(barrier, 6)
    pack_copies = sends(pack_send, pack_recv, 0)
    for c in pack_copies:
        c.start()

    def count_rows(tile, first_slot, base):
        rows = 32
        where = iota((rows, ATOMS_DEV), 0) + (tile * rows + base)
        total = jnp.zeros((rows, ATOMS_DEV), F32)
        for s in range(first_slot, first_slot + SLOTS_HALF):
            total = total + jnp.where(nbr_ref[s : s + 1, :] == where, 1.0, 0.0)
        count[pl.ds(pl.multiple_of(tile * rows + base, rows), rows), :] = total

    @pl.loop(0, ATOMS_DEV // 32)
    def _(tile):
        count_rows(tile, 0, 0)

    @pl.loop(0, GHOSTS // 32)
    def _(tile):
        count_rows(tile, SLOTS_HALF, ATOMS_DEV)

    centre = own[0:3]

    def radial_rows(tile, base):
        rows = 32
        place = pl.ds(pl.multiple_of(tile * rows + base, rows), rows)
        squared = None
        for c in range(3):
            gap = col[place, c : c + 1] - pos_ref[c : c + 1, :]
            squared = gap * gap if squared is None else squared + gap * gap
        scaled = squared * (2.0 * ROOT_LOG2E)
        times = count[place, :]
        for k in range(KB):
            off = scaled - ROOT_LOG2E * k
            rad[k, place, :] = (jnp.exp2(-(off * off)) * times).astype(BF16)

    def left_rows(packed):
        n = packed.shape[1]
        eight = iota((8, n), 0).astype(F32)
        hot_low = jnp.where(packed[3:4] == eight, 1.0, 0.0)
        hot_high = jnp.where(packed[3:4] == eight - 4.0, 1.0, 0.0)
        p_high, p_low = split(packed[0:3])
        place = jnp.concatenate([p_high, p_low, jnp.zeros((2, n), F32)], axis=0)
        blank = jnp.zeros((8, n), F32)
        even = jnp.concatenate([jnp.where(eight < 4.0, hot_low, 0.0), place, blank, blank], axis=0)
        odd = jnp.concatenate([jnp.where(eight < 4.0, 0.0, hot_high), blank, place, blank], axis=0)
        return even.astype(BF16), odd.astype(BF16), jnp.where(eight < 4.0, hot_low, 0.0)

    def gather_sums(even, odd, first, rows):
        part = []
        for q in range(4):
            part.append(
                dot(even, rad[2 * q, first : first + rows, :])
                + dot(odd, rad[2 * q + 1, first : first + rows, :])
            )
        return part

    col[0:ATOMS_DEV, :] = own.T

    @pl.loop(0, ATOMS_DEV // 32)
    def _(tile):
        radial_rows(tile, 0)

    even_own, odd_own, hot_own = left_rows(own)
    sums = gather_sums(even_own, odd_own, 0, ATOMS_DEV)

    filt = filt_ref[...].astype(F32)
    emb = emb_ref[...].astype(F32)
    emb8 = jnp.concatenate([emb, emb], axis=0)
    upper = iota((8, WIDTH), 0) < 4
    first_w = jnp.concatenate(
        [
            SCALE * emb8 * jnp.where(upper, filt[0, 2 * q : 2 * q + 1], filt[0, 2 * q + 1 : 2 * q + 2])
            for q in range(4)
        ],
        axis=0,
    )
    w_high, w_low = split(first_w)
    w_msg[...] = jnp.concatenate([w_high, w_high, w_low, jnp.zeros((32, WIDTH), F32)], axis=0).T.astype(BF16)
    w_emb[...] = jnp.concatenate(
        [jnp.zeros((96, WIDTH), F32), jnp.where(upper, emb8, 0.0), jnp.zeros((24, WIDTH), F32)], axis=0
    ).T.astype(BF16)
    filt_t = (SCALE * filt[1]).T
    for k in range(KB):
        fbc[k] = jnp.broadcast_to(filt_t[:, k : k + 1], (WIDTH, 128))
    u_copy.wait()
    v_copy.wait()
    for l in range(2):
        for m in range(MODELS):
            uvt[l, m, :, 0:128] = u_vm[l, m].astype(F32).T.astype(BF16)
            uvt[l, m, :, 128:256] = v_vm[l, m].astype(F32).T.astype(BF16)

    for c in pack_copies:
        c.wait_recv()
    lane_low = iota((8, 128), 1) < 64
    sub = iota((8, 128), 0)
    tiles = [
        pack_recv[0] - jnp.where(sub == 0, 1.0, 0.0),
        pack_recv[1] + jnp.where(sub == 0, 1.0, 0.0),
    ]
    for axis in (1, 2):
        step = jnp.where(sub == axis, 1.0, 0.0)
        tiles.append(
            jnp.where(lane_low, pack_recv[2 * axis] - step, pack_recv[2 * axis + 1] + step)
        )
    lent = jnp.concatenate(tiles, axis=1)
    col[ATOMS_DEV:TABLE, :] = lent.T

    @pl.loop(0, GHOSTS // 32)
    def _(tile):
        radial_rows(tile, ATOMS_DEV)

    even_lent, odd_lent, hot_lent = left_rows(lent)
    more = gather_sums(even_lent, odd_lent, ATOMS_DEV, GHOSTS)
    sums = [a + b for a, b in zip(sums, more)]

    agg = jnp.concatenate([s[0:8] for s in sums], axis=0)
    a_high, a_low = split(agg)
    chosen = dot(jnp.concatenate([a_high, a_low], axis=0).astype(BF16), sel[...])
    chosen = chosen[0:32] + chosen[32:64]
    for g in range(4):
        agg_send[g] = chosen[:, g * 128 : (g + 1) * 128]
    agg_copies = sends(agg_send, agg_recv, 6)
    for c in agg_copies:
        c.start()

    for q in range(4):
        for odd in range(2):
            k = 2 * q + odd
            weight = jnp.sum(sums[q][4 * odd : 4 * odd + 4], axis=0, keepdims=True)
            base = 8 + 8 * odd
            for c in range(3):
                dsum[c, k : k + 1, :] = (
                    sums[q][base + c : base + c + 1]
                    + sums[q][base + 3 + c : base + 4 + c]
                    - centre[c : c + 1] * weight
                )

    def first_layer(table, hot):
        n = table.shape[1]
        t_high, t_low = split(table)
        x = jnp.concatenate([t_high, t_low, t_high, hot, jnp.zeros((24, n), F32)], axis=0).astype(BF16)
        result = []
        for m in range(MODELS):
            rows = slice(m * C, (m + 1) * C)
            msg = dot(w_msg[rows, :], x).astype(BF16)
            h = dot(w_emb[rows, :], x)
            pre = dot(uvt[0, m], jnp.concatenate([msg, h.astype(BF16)], axis=0))
            result.append(add_silu(h, pre))
        return result

    for m, h in enumerate(first_layer(agg, hot_own)):
        h_own[m * C : (m + 1) * C, :] = h
        h_tab[m * C : (m + 1) * C, 0:ATOMS_DEV] = h.astype(BF16)

    def second_messages(first, rows, begin):
        for k in range(KB):
            part = dot(h_tab[:, first : first + rows], rad[k, first : first + rows, :])
            for half in range(2):
                lanes = slice(half * 128, (half + 1) * 128)
                scaled = fbc[k] * part[:, lanes]
                acc[:, lanes] = scaled if begin and k == 0 else acc[:, lanes] + scaled

    second_messages(0, ATOMS_DEV, True)

    for c in agg_copies:
        c.wait_recv()
    wide_low = iota((32, 128), 1) < 64
    tables = [agg_recv[0], agg_recv[1]]
    for axis in (1, 2):
        tables.append(jnp.where(wide_low, agg_recv[2 * axis], agg_recv[2 * axis + 1]))
    for m, h in enumerate(first_layer(jnp.concatenate(tables, axis=1), hot_lent)):
        h_tab[m * C : (m + 1) * C, ATOMS_DEV:TABLE] = h.astype(BF16)
    second_messages(ATOMS_DEV, GHOSTS, False)

    forces = []
    for m in range(MODELS):
        rows = slice(m * C, (m + 1) * C)
        x = jnp.concatenate([acc[rows, :].astype(BF16), h_tab[rows, 0:ATOMS_DEV]], axis=0)
        h = add_silu(h_own[rows, :], dot(uvt[1, m], x))
        coeff = dot(fw_ref[m], h.astype(BF16))
        forces.append([SCALE * jnp.sum(coeff * dsum[c], axis=0, keepdims=True) for c in range(3)])
    alive = jnp.where(iota((1, ATOMS_DEV), 1) < live_ref[...], 1.0, 0.0)
    spread = jnp.zeros((1, ATOMS_DEV), F32)
    for c in range(3):
        mean = (forces[0][c] + forces[1][c] + forces[2][c] + forces[3][c]) * 0.25
        for m in range(MODELS):
            gap = forces[m][c] - mean
            spread = spread + gap * gap
        mean_ref[c : c + 1, :] = mean * alive
    dev_ref[...] = spread * 0.25 * alive

    for c in pack_copies + agg_copies:
        c.wait_send()


def solution(mesh):
    sizes = tuple(mesh.shape[a] for a in AXES)

    def local(positions, species, neighbors, atom_count, ghost_x, ghost_yz, embedding, filters, update_u, update_v, force_w):
        vmem = pl.BlockSpec(memory_space=pltpu.VMEM)
        anywhere = pl.BlockSpec(memory_space=pl.ANY)
        mean, spread = pl.pallas_call(
            functools.partial(kernel, sizes),
            out_shape=(
                jax.ShapeDtypeStruct((3, ATOMS_DEV), F32),
                jax.ShapeDtypeStruct((1, ATOMS_DEV), F32),
            ),
            in_specs=[vmem, vmem, vmem, vmem, vmem, vmem, vmem, vmem, anywhere, anywhere, vmem],
            out_specs=(vmem, vmem),
            scratch_shapes=[
                pltpu.VMEM((ATOMS_DEV, GHOSTS), BF16),
                pltpu.VMEM((4, 8, 128), F32),
                pltpu.VMEM((6, 8, 128), F32),
                pltpu.VMEM((4, 32, 128), F32),
                pltpu.VMEM((6, 32, 128), F32),
                pltpu.VMEM((TABLE, ATOMS_DEV), F32),
                pltpu.VMEM((TABLE, 8), F32),
                pltpu.VMEM((KB, TABLE, ATOMS_DEV), BF16),
                pltpu.VMEM((8, 128), F32),
                pltpu.VMEM((8, 128), F32),
                pltpu.VMEM((WIDTH, ATOMS_DEV), F32),
                pltpu.VMEM((WIDTH, TABLE), BF16),
                pltpu.VMEM((WIDTH, ATOMS_DEV), F32),
                pltpu.VMEM((KB, WIDTH, 128), F32),
                pltpu.VMEM((2, MODELS, C, 2 * C), BF16),
                pltpu.VMEM((WIDTH, 128), BF16),
                pltpu.VMEM((WIDTH, 128), BF16),
                pltpu.VMEM((3, KB, ATOMS_DEV), F32),
                pltpu.VMEM((2, MODELS, C, C), BF16),
                pltpu.VMEM((2, MODELS, C, C), BF16),
                pltpu.SemaphoreType.DMA((12,)),
                pltpu.SemaphoreType.DMA((12,)),
                pltpu.SemaphoreType.DMA((2,)),
            ],
            compiler_params=pltpu.CompilerParams(
                collective_id=0, has_side_effects=True, vmem_limit_bytes=60 * 1024 * 1024
            ),
        )(
            positions,
            species.reshape(1, ATOMS_DEV),
            neighbors,
            atom_count.reshape(1, 1),
            ghost_x.reshape(2, 2 * 64),
            ghost_yz.reshape(4, 64),
            embedding,
            filters,
            update_u,
            update_v,
            jnp.swapaxes(force_w, 1, 2),
        )
        return mean, spread.reshape(ATOMS_DEV)

    split_spec = P(AXES)
    return jax.shard_map(
        local,
        mesh=mesh,
        in_specs=(
            P(None, AXES), split_spec, P(None, AXES), split_spec,
            P(AXES, None, None), P(AXES, None, None), P(), P(), P(), P(), P(),
        ),
        out_specs=(P(None, AXES), split_spec),
        check_vma=False,
    )
```

time: 449 us -> 27.1 us (0.06); the launches traced: 440 us -> 26.9 us
  local copies, waits for them, and re-layouts: 259 us -> 1.87 us
  matrix products: 79.4 us -> 0 us
  starting transfers between devices: 46.6 us -> 0 us
  waiting for transfers between devices: 31.6 us -> 0 us
  Pallas kernels: 0 us -> 23.8 us
  other arithmetic: 19.7 us -> 0 us
    gather x70 -> x0, local copies, waits for them, and re-layouts: 236 us -> none  [the longest x32 156 us: message(): summed = summed + jnp.sum(weights * feat_table[group_ids], axis=0)]
    dot_general x46 -> x0, matrix products: 79.4 us -> none  [the longest x32 67.6 us: message(): weights = jnp.einsum('ksr,kc->src', radial_g, filter_w)]
    ppermute x30 -> x0, starting transfers between devices: 46.6 us -> none  [from_behind(): return lax.ppermute(x, axis, [(i, (i + by) % peers) for i in range(peers)])]
    ppermute x30 -> x0, waiting for transfers between devices: 31.6 us -> none  [from_behind(): return lax.ppermute(x, axis, [(i, (i + by) % peers) for i in range(peers)])]
    pallas_call x0 -> x1, Pallas kernels: none -> 23.8 us  [local(): pl.pallas_call(functools.partial(kernel, sizes), out_shape=(jax.ShapeDtyp...]
    convert_element_type x10 -> x0, local copies, waits for them, and re-layouts: 8.84 us -> none  [the longest x4 4.35 us: refresh(): summed_messages.astype(jnp.bfloat16).reshape(rows_n, models, width_c)]
    while x34 -> x0, local copies, waits for them, and re-layouts: 5.35 us -> none
    convert_element_type x11 -> x0, other arithmetic: 4.96 us -> none  [the longest x4 3.39 us: refresh(): summed_messages.astype(jnp.bfloat16).reshape(rows_n, models, width_c)]
  transfers between devices with their start and end apart: 30 -> 0, of which waited for: 9 -> 0; matrix products, arithmetic and copies ran while one was open for 3% -> 0% of each run, Pallas kernels for 0% -> 0%
where the time goes in v1:
time: 27.1 us; the launch traced here: 26.9 us
  Pallas kernels  23.8 us (88%)
  local copies, waits for them, and re-layouts  1.87 us (7%)
  between operations  1.3 us (5%)
    pallas_call x1, Pallas kernels, local(): pl.pallas_call(functools.partial(kernel, sizes), out_shape=(jax.ShapeDtyp...  23.8 us
    unnamed x6, local copies, waits for them, and re-layouts  1.87 us

profile of v1, /device:TPU:6, one launch (start us, length us, event | category | flops | bytes accessed | tf_op | source)
XLA Modules:
  0.0 26.9 jit_solution(14253657586845901765)
XLA Ops:
  1.3 23.8 %shard_map.122 = (f32[3,256]{1,0:T(4,128)}, f32[1,256]{1,0:T(1,128)}) custom-call(f32[3,256]{1,0:T(4,128)} %pos_ref.1, s32[1,256]{1,0:T(1,128)} %bitcast.9, s32[64,256]{1,0:T(8,128)} %nbr_ref.1, s32[1,1]{1,0:T(1,128)} %bitcast.6.live_ref, s32[2,128]{1,0:T(2,128)} %bitcast.10, s32[4,64]{1,0:T(4,128)} %bitcast.8, bf16[4,512]{1,0:T(4,128)(2,1)} %emb_ref.1, ...), custom_call_target="tpu_custom_call" | custom-call | tf_op jit(solution)/shard_map/pallas_call | solution.py:300
  25.1 0.0 copy-start
  25.1 0.7 %copy-done = f32[3,256]{1,0:T(4,128)S(1)} copy-done((f32[3,256]{1,0:T(4,128)S(1)}, f32[3,256]{1,0:T(4,128)}, u32[]{:S(2)}) %copy-start) | copy-done | bytes 3096
  25.7 0.0 copy-start.1
  25.7 0.6 %copy.16 = f32[3,256]{1,0:T(4,128)} copy(f32[3,256]{1,0:T(4,128)S(1)} %copy-done) | data formatting | bytes 6144
  26.3 0.0 copy-done.1
  26.4 0.6 %copy.17 = f32[256]{0:T(256)} copy(f32[256]{0:T(256)S(1)} %bitcast.11) | data formatting | bytes 2048
Async XLA Ops:
  25.1 0.7 %copy-start = (f32[3,256]{1,0:T(4,128)S(1)}, f32[3,256]{1,0:T(4,128)}, u32[]{:S(2)}) copy-start(f32[3,256]{1,0:T(4,128)} %get-tuple-element.8) | copy-start | bytes 9220
  25.7 0.6 %copy-start.1 = (f32[1,256]{1,0:T(1,128)S(1)}, f32[1,256]{1,0:T(1,128)}, u32[]{:S(2)}) copy-start(f32[1,256]{1,0:T(1,128)} %get-tuple-element.5) | copy-start | bytes 3076

commit v2 on v1

v2 whole, which is shorter than its diff:
```python
import functools

import jax
import jax.numpy as jnp
from jax import lax
from jax.experimental import pallas as pl
from jax.experimental.pallas import tpu as pltpu
from jax.sharding import PartitionSpec as P

ATOMS_DEV = 256
GHOSTS = 512
TABLE = ATOMS_DEV + GHOSTS
MODELS = 4
C = 128
WIDTH = MODELS * C
KB = 8
SPECIES = 4
SLOTS_HALF = 32
SCALE = 0.125
ROOT_LOG2E = 1.2011224087864498
F32 = jnp.float32
BF16 = jnp.bfloat16
AXES = ("gx", "gy", "gz")


def iota(shape, dim):
    return lax.broadcasted_iota(jnp.int32, shape, dim)


def dot(a, b):
    return lax.dot_general(a, b, (((1,), (0,)), ((), ())), preferred_element_type=F32)


def split(x):
    high = x.astype(BF16).astype(F32)
    return high, (x - high).astype(BF16).astype(F32)


def add_silu(h, pre):
    half = 0.5 * pre
    return h + half + half * jnp.tanh(half)


LOG2E = 1.4426950408889634
DROP = 0.1353352832366127


def kernel(
    sizes,
    pos_hbm, spec_hbm, nbr_hbm, live_hbm, gx_hbm, gyz_hbm, emb_ref, filt_ref, u_hbm, v_hbm, fw_ref,
    mean_ref, dev_ref,
    pos_ref, spec_ref, nbr_ref, live_ref, gx_ref, gyz_ref, u_vm, v_vm,
    sel, pack_send, pack_recv, agg_send, agg_recv, slots, count, col, rad, h_own, h_tab, acc,
    fbc, uvt, w_msg, w_emb, dsum, sent,
    send_sem, recv_sem, copy_sem,
):
    here = [lax.axis_index(a) for a in AXES]
    odd_x = lax.rem(here[0], 2)
    step_x = 1 - 2 * odd_x
    def peer(number, step):
        size = sizes[number]
        return {AXES[number]: lax.rem(here[number] + step + size, size)}

    peers = [peer(2, 1), peer(2, -1), peer(0, step_x), peer(0, -step_x), peer(1, 1), peer(1, -1)]

    barrier = pltpu.get_barrier_semaphore()
    for target in peers:
        pl.semaphore_signal(barrier, inc=1, device_id=target, device_id_type=pl.DeviceIdType.MESH)
    loads = [
        pltpu.make_async_copy(source, target, copy_sem.at[n])
        for n, (source, target) in enumerate(
            (
                (gx_hbm, gx_ref), (gyz_hbm, gyz_ref), (pos_hbm, pos_ref), (spec_hbm, spec_ref),
                (nbr_hbm, nbr_ref), (u_hbm, u_vm), (v_hbm, v_vm), (live_hbm, live_ref),
            )
        )
    ]
    for c in loads:
        c.start()
    for c in loads[0:4]:
        c.wait()

    lists = [
        jnp.concatenate([gyz_ref[2:3, :], gyz_ref[3:4, :]], axis=1),
        gx_ref[pl.ds(odd_x, 1), :],
        gx_ref[pl.ds(1 - odd_x, 1), :],
        jnp.concatenate([gyz_ref[0:1, :], gyz_ref[1:2, :]], axis=1),
    ]
    atom_row = iota((ATOMS_DEV, 128), 0)
    for g in range(4):
        sel[:, g * 128 : (g + 1) * 128] = jnp.where(atom_row == lists[g], 1.0, 0.0).astype(BF16)

    own = jnp.concatenate(
        [pos_ref[...], spec_ref[...].astype(F32), jnp.zeros((4, ATOMS_DEV), F32)], axis=0
    )
    high = own.astype(BF16).astype(F32)
    rest = own - high
    middle = rest.astype(BF16).astype(F32)
    low = rest - middle
    picked = dot(jnp.concatenate([high, middle, low], axis=0).astype(BF16), sel[...])
    picked = picked[0:8] + picked[8:16] + picked[16:24]
    for g in range(4):
        pack_send[g] = picked[:, g * 128 : (g + 1) * 128]

    def sends(source, target, first):
        return [
            pltpu.make_async_remote_copy(
                src_ref=source.at[group],
                dst_ref=target.at[face],
                send_sem=send_sem.at[first + face],
                recv_sem=recv_sem.at[first + face],
                device_id=peers[face],
                device_id_type=pl.DeviceIdType.MESH,
            )
            for face, group in enumerate((0, 0, 1, 2, 3, 3))
        ]

    pl.semaphore_wait(barrier, 6)
    pack_copies = sends(pack_send, pack_recv, 0)
    for n in (3, 4, 5, 0, 1, 2):
        pack_copies[n].start()

    loads[4].wait()
    for s in range(SLOTS_HALF):
        slots[s] = jnp.broadcast_to(nbr_ref[s : s + 1, :].astype(F32), (16, ATOMS_DEV)).astype(BF16)
        lent_id = jnp.broadcast_to(nbr_ref[SLOTS_HALF + s : SLOTS_HALF + s + 1, :].astype(F32), (16, ATOMS_DEV))
        slots[SLOTS_HALF + s] = (lent_id - 256.0).astype(BF16)
        slots[2 * SLOTS_HALF + s] = (lent_id - 512.0).astype(BF16)

    one = jnp.ones((16, ATOMS_DEV), BF16)
    nil = jnp.zeros((16, ATOMS_DEV), BF16)

    def count_rows(first_slot, base, first_row, rows):
        @pl.loop(0, rows // 64)
        def _(tile):
            which = [
                (iota((16, ATOMS_DEV), 0) + (tile * 64 + base + 16 * r)).astype(F32).astype(BF16)
                for r in range(4)
            ]
            total = [nil] * 4
            for s in range(first_slot, first_slot + SLOTS_HALF):
                ids = slots[s]
                total = [t + jnp.where(ids == w, one, nil) for t, w in zip(total, which)]
            for r in range(4):
                place = pl.ds(pl.multiple_of(tile * 64 + (first_row + 16 * r), 16), 16)
                count[place, :] = total[r]

    count_rows(0, 0, 0, 256)
    count_rows(2 * SLOTS_HALF, 128, 256, 128)
    count_rows(SLOTS_HALF, 128 * (1 - odd_x), 384, 128)
    count_rows(SLOTS_HALF, 128 * odd_x, 512, 128)
    count_rows(2 * SLOTS_HALF, 0, 640, 128)

    centre = own[0:3]

    def radial_rows(part):
        rows = 32
        for tile in range(256 // rows):
            first = part * 256 + tile * rows
            squared = None
            for c in range(3):
                gap = col[first : first + rows, c : c + 1] - pos_ref[c : c + 1, :]
                squared = gap * gap if squared is None else squared + gap * gap
            off = squared * (2.0 * ROOT_LOG2E) - 4.0 * ROOT_LOG2E
            grow = squared * (4.0 * LOG2E)
            up = jnp.exp2(grow - 9.0 * LOG2E)
            down = jnp.exp2(7.0 * LOG2E - grow)
            mid = jnp.exp2(-(off * off)) * count[first : first + rows, :].astype(F32)

            def put(k, value):
                rad[part, k * 256 + tile * rows : k * 256 + (tile + 1) * rows, :] = value.astype(BF16)

            put(4, mid)
            value = mid
            for k in (5, 6, 7):
                value = value * up
                put(k, value)
                up = up * DROP
            value = mid
            for k in (3, 2, 1, 0):
                value = value * down
                put(k, value)
                down = down * DROP

    def left_rows(packed):
        n = packed.shape[1]
        eight = iota((8, n), 0).astype(F32)
        hot = jnp.where(packed[3:4] == eight, 1.0, 0.0)
        hot_high = jnp.where(packed[3:4] == eight - 4.0, 1.0, 0.0)
        p_high, p_low = split(packed[0:3])
        place = jnp.concatenate([p_high, p_low, jnp.zeros((2, n), F32)], axis=0)
        blank = jnp.zeros((8, n), F32)
        even = jnp.concatenate([hot, place, blank, blank], axis=0)
        odd = jnp.concatenate([hot_high, blank, place, blank], axis=0)
        return jnp.concatenate([even.astype(BF16), odd.astype(BF16)], axis=1), hot

    def gather_sums(both, part):
        return [dot(both, rad[part, q * 512 : (q + 1) * 512, :]) for q in range(4)]

    col[0:256, :] = own.T
    radial_rows(0)
    both_own, hot_own = left_rows(own)
    for q, s in enumerate(gather_sums(both_own, 0)):
        sent[q] = s

    filt = filt_ref[...].astype(F32)
    emb = emb_ref[...].astype(F32)
    emb8 = jnp.concatenate([emb, emb], axis=0)
    upper = iota((8, WIDTH), 0) < 4
    first_w = jnp.concatenate(
        [
            SCALE * emb8 * jnp.where(upper, filt[0, 2 * q : 2 * q + 1], filt[0, 2 * q + 1 : 2 * q + 2])
            for q in range(4)
        ],
        axis=0,
    )
    w_high, w_low = split(first_w)
    w_msg[...] = jnp.concatenate([w_high, w_high, w_low, jnp.zeros((32, WIDTH), F32)], axis=0).T.astype(BF16)
    w_emb[...] = jnp.concatenate(
        [jnp.zeros((96, WIDTH), F32), jnp.where(upper, emb8, 0.0), jnp.zeros((24, WIDTH), F32)], axis=0
    ).T.astype(BF16)
    filt_t = (SCALE * filt[1]).T
    for k in range(KB):
        fbc[k] = jnp.broadcast_to(filt_t[:, k : k + 1], (WIDTH, 128)).astype(BF16)
    loads[5].wait()
    loads[6].wait()
    for l in range(2):
        for m in range(MODELS):
            uvt[l, m, :, 0:128] = u_vm[l, m].astype(F32).T.astype(BF16)
            uvt[l, m, :, 128:256] = v_vm[l, m].astype(F32).T.astype(BF16)

    lane_low = iota((8, 128), 1) < 64
    sub = iota((8, 128), 0)

    def pair(first, axis):
        step = jnp.where(sub == axis, 1.0, 0.0)
        return jnp.where(lane_low, pack_recv[first] - step, pack_recv[first + 1] + step)

    near = jnp.where(sub == 0, step_x.astype(F32), 0.0)
    for c in pack_copies[0:3]:
        c.wait_recv()
    early = jnp.concatenate([pair(0, 2), pack_recv[2] + near], axis=1)
    col[256:512, :] = early.T
    radial_rows(1)
    both_early, hot_early = left_rows(early)
    for q, s in enumerate(gather_sums(both_early, 1)):
        sent[q] = sent[q] + s

    for c in pack_copies[3:6]:
        c.wait_recv()
    late = jnp.concatenate([pack_recv[3] - near, pair(4, 1)], axis=1)
    col[512:768, :] = late.T
    radial_rows(2)
    both_late, hot_late = left_rows(late)
    sums = [sent[q] + s for q, s in enumerate(gather_sums(both_late, 2))]

    agg = jnp.concatenate([s[0:8] for s in sums], axis=0)
    a_high, a_low = split(agg)
    chosen = dot(jnp.concatenate([a_high, a_low], axis=0).astype(BF16), sel[...])
    chosen = chosen[0:32] + chosen[32:64]
    for g in range(4):
        agg_send[g] = chosen[:, g * 128 : (g + 1) * 128]
    agg_copies = sends(agg_send, agg_recv, 6)
    for n in (3, 4, 5, 0, 1, 2):
        agg_copies[n].start()

    for q in range(4):
        for odd in range(2):
            k = 2 * q + odd
            weight = jnp.sum(sums[q][4 * odd : 4 * odd + 4], axis=0, keepdims=True)
            base = 8 + 8 * odd
            for c in range(3):
                dsum[c, k : k + 1, :] = (
                    sums[q][base + c : base + c + 1]
                    + sums[q][base + 3 + c : base + 4 + c]
                    - centre[c : c + 1] * weight
                )

    def first_layer(table, hot):
        n = table.shape[1]
        t_high, t_low = split(table)
        x = jnp.concatenate([t_high, t_low, t_high, hot, jnp.zeros((24, n), F32)], axis=0).astype(BF16)
        result = []
        for m in range(MODELS):
            rows = slice(m * C, (m + 1) * C)
            msg = dot(w_msg[rows, :], x).astype(BF16)
            h = dot(w_emb[rows, :], x)
            pre = dot(uvt[0, m], jnp.concatenate([msg, h.astype(BF16)], axis=0))
            result.append(add_silu(h, pre))
        return result

    def weigh(m, h):
        rows = slice(m * C, (m + 1) * C)
        for k in range(KB):
            for half in range(2):
                lanes = slice(half * 128, (half + 1) * 128)
                h_tab[rows, k * 256 + half * 128 : k * 256 + (half + 1) * 128] = h[:, lanes] * fbc[k, rows, :]

    for m, h in enumerate(first_layer(agg, hot_own)):
        h_own[m * C : (m + 1) * C, :] = h
        weigh(m, h.astype(BF16))
    acc[...] = dot(h_tab[...], rad[0])

    wide_low = iota((32, 128), 1) < 64

    def agg_pair(first):
        return jnp.where(wide_low, agg_recv[first], agg_recv[first + 1])

    for c in agg_copies[0:3]:
        c.wait_recv()
    for m, h in enumerate(first_layer(jnp.concatenate([agg_pair(0), agg_recv[2]], axis=1), hot_early)):
        weigh(m, h.astype(BF16))
    acc[...] += dot(h_tab[...], rad[1])
    for c in agg_copies[3:6]:
        c.wait_recv()
    for m, h in enumerate(first_layer(jnp.concatenate([agg_recv[3], agg_pair(4)], axis=1), hot_late)):
        weigh(m, h.astype(BF16))
    message = (acc[...] + dot(h_tab[...], rad[2])).astype(BF16)

    forces = []
    for m in range(MODELS):
        rows = slice(m * C, (m + 1) * C)
        x = jnp.concatenate([message[rows], h_own[rows, :].astype(BF16)], axis=0)
        h = add_silu(h_own[rows, :], dot(uvt[1, m], x))
        coeff = dot(fw_ref[m], h.astype(BF16))
        forces.append([SCALE * jnp.sum(coeff * dsum[c], axis=0, keepdims=True) for c in range(3)])
    loads[7].wait()
    alive = jnp.where(iota((1, ATOMS_DEV), 1) < live_ref[...], 1.0, 0.0)
    spread = jnp.zeros((1, ATOMS_DEV), F32)
    for c in range(3):
        mean = (forces[0][c] + forces[1][c] + forces[2][c] + forces[3][c]) * 0.25
        for m in range(MODELS):
            gap = forces[m][c] - mean
            spread = spread + gap * gap
        mean_ref[c : c + 1, :] = mean * alive
    dev_ref[...] = spread * 0.25 * alive

    for c in pack_copies + agg_copies:
        c.wait_send()


def solution(mesh):
    sizes = tuple(mesh.shape[a] for a in AXES)

    def local(positions, species, neighbors, atom_count, ghost_x, ghost_yz, embedding, filters, update_u, update_v, force_w):
        vmem = pl.BlockSpec(memory_space=pltpu.VMEM)
        anywhere = pl.BlockSpec(memory_space=pl.ANY)
        mean, spread = pl.pallas_call(
            functools.partial(kernel, sizes),
            out_shape=(pltpu.VMEM((3, ATOMS_DEV), F32), pltpu.VMEM((1, ATOMS_DEV), F32)),
            in_specs=[anywhere] * 6 + [vmem, vmem, anywhere, anywhere, vmem],
            out_specs=(vmem, vmem),
            scratch_shapes=[
                pltpu.VMEM((3, ATOMS_DEV), F32),
                pltpu.VMEM((1, ATOMS_DEV), jnp.int32),
                pltpu.VMEM((2 * SLOTS_HALF, ATOMS_DEV), jnp.int32),
                pltpu.VMEM((1, 1), jnp.int32),
                pltpu.VMEM((2, 128), jnp.int32),
                pltpu.VMEM((4, 64), jnp.int32),
                pltpu.VMEM((2, MODELS, C, C), BF16),
                pltpu.VMEM((2, MODELS, C, C), BF16),
                pltpu.VMEM((ATOMS_DEV, GHOSTS), BF16),
                pltpu.VMEM((4, 8, 128), F32),
                pltpu.VMEM((6, 8, 128), F32),
                pltpu.VMEM((4, 32, 128), F32),
                pltpu.VMEM((6, 32, 128), F32),
                pltpu.VMEM((3 * SLOTS_HALF, 16, ATOMS_DEV), BF16),
                pltpu.VMEM((TABLE, ATOMS_DEV), BF16),
                pltpu.VMEM((TABLE, 8), F32),
                pltpu.VMEM((3, KB * 256, ATOMS_DEV), BF16),
                pltpu.VMEM((WIDTH, ATOMS_DEV), F32),
                pltpu.VMEM((WIDTH, KB * 256), BF16),
                pltpu.VMEM((WIDTH, ATOMS_DEV), F32),
                pltpu.VMEM((KB, WIDTH, 128), BF16),
                pltpu.VMEM((2, MODELS, C, 2 * C), BF16),
                pltpu.VMEM((WIDTH, 128), BF16),
                pltpu.VMEM((WIDTH, 128), BF16),
                pltpu.VMEM((3, KB, ATOMS_DEV), F32),
                pltpu.VMEM((4, 32, ATOMS_DEV), F32),
                pltpu.SemaphoreType.DMA((12,)),
                pltpu.SemaphoreType.DMA((12,)),
                pltpu.SemaphoreType.DMA((8,)),
            ],
            compiler_params=pltpu.CompilerParams(
                collective_id=0, has_side_effects=True, vmem_limit_bytes=60 * 1024 * 1024
            ),
        )(
            positions,
            species.reshape(1, ATOMS_DEV),
            neighbors,
            atom_count.reshape(1, 1),
            ghost_x.reshape(2, 2 * 64),
            ghost_yz.reshape(4, 64),
            embedding,
            filters,
            update_u,
            update_v,
            jnp.swapaxes(force_w, 1, 2),
        )
        return mean, spread.reshape(ATOMS_DEV)

    split_spec = P(AXES)
    return jax.shard_map(
        local,
        mesh=mesh,
        in_specs=(
            P(None, AXES), split_spec, P(None, AXES), split_spec,
            P(AXES, None, None), P(AXES, None, None), P(), P(), P(), P(), P(),
        ),
        out_specs=(P(None, AXES), split_spec),
        check_vma=False,
    )
```

time: 27.1 us -> 23.8 us (0.88)
  the two profiles are of different devices: /device:TPU:6 before, /device:TPU:2 now
where the time goes in v2:
time: 23.8 us; the launch traced here: 23.5 us
  Pallas kernels  21.1 us (89%)
  between operations  1.29 us (5%)
  local copies, waits for them, and re-layouts  1.16 us (5%)
    pallas_call x1, Pallas kernels, local(): pl.pallas_call(functools.partial(kernel, sizes), out_shape=(pltpu.VMEM((3...  21.1 us
    unnamed x2, local copies, waits for them, and re-layouts  1.16 us

profile of v2, /device:TPU:2, one launch (start us, length us, event | category | flops | bytes accessed | tf_op | source)
XLA Modules:
  0.0 23.5 jit_solution(14307260739045626881)
XLA Ops:
  1.3 21.1 %shard_map.122 = (f32[3,256]{1,0:T(4,128)S(1)}, f32[1,256]{1,0:T(1,128)S(1)}) custom-call(f32[3,256]{1,0:T(4,128)} %pos_hbm.1, s32[1,256]{1,0:T(1,128)} %bitcast.10, s32[64,256]{1,0:T(8,128)} %nbr_hbm.1, s32[1,1]{1,0:T(1,128)} %bitcast.6.live_hbm, s32[2,128]{1,0:T(2,128)} %bitcast.11, s32[4,64]{1,0:T(4,128)} %bitcast.9, bf16[4,512]{1,0:T(4,128)(2,1)} %emb_ref.1, ...), custom_call_target="tpu_custom_call" | custom-call | tf_op jit(solution)/shard_map/pallas_call | solution.py:348
  22.4 0.6 %copy.15 = f32[3,256]{1,0:T(4,128)} copy(f32[3,256]{1,0:T(4,128)S(1)} %get-tuple-element.6) | data formatting | bytes 6144
  23.0 0.6 %copy.16 = f32[256]{0:T(256)} copy(f32[256]{0:T(256)S(1)} %bitcast.7) | data formatting | bytes 2048

commit v3 on v2

--- a/solution.py
+++ b/solution.py
@@ -47,11 +47,11 @@
 
 def kernel(
     sizes,
-    pos_hbm, spec_hbm, nbr_hbm, live_hbm, gx_hbm, gyz_hbm, emb_ref, filt_ref, u_hbm, v_hbm, fw_ref,
+    pos_hbm, spec_hbm, nbr_hbm, live_hbm, gx_hbm, gyz_hbm, emb_hbm, filt_hbm, u_hbm, v_hbm, fw_hbm,
     mean_ref, dev_ref,
-    pos_ref, spec_ref, nbr_ref, live_ref, gx_ref, gyz_ref, u_vm, v_vm,
+    pos_ref, spec_ref, nbr_ref, live_ref, gx_ref, gyz_ref, u_vm, v_vm, emb_ref, filt_ref, fw_ref,
     sel, pack_send, pack_recv, agg_send, agg_recv, slots, count, col, rad, h_own, h_tab, acc,
-    fbc, uvt, w_msg, w_emb, dsum, sent,
+    fbc, uvt, w_msg, dsum, sent,
     send_sem, recv_sem, copy_sem,
 ):
     here = [lax.axis_index(a) for a in AXES]
@@ -71,7 +71,7 @@
         for n, (source, target) in enumerate(
             (
                 (gx_hbm, gx_ref), (gyz_hbm, gyz_ref), (pos_hbm, pos_ref), (spec_hbm, spec_ref),
-                (nbr_hbm, nbr_ref), (u_hbm, u_vm), (v_hbm, v_vm), (live_hbm, live_ref),
+                (nbr_hbm, nbr_ref), (emb_hbm, emb_ref), (filt_hbm, filt_ref), (u_hbm, u_vm), (v_hbm, v_vm), (fw_hbm, fw_ref), (live_hbm, live_ref),
             )
         )
     ]
@@ -203,6 +203,43 @@
     for q, s in enumerate(gather_sums(both_own, 0)):
         sent[q] = s
 
+    lane_low = iota((8, 128), 1) < 64
+    sub = iota((8, 128), 0)
+
+    def pair(first, axis):
+        step = jnp.where(sub == axis, 1.0, 0.0)
+        return jnp.where(lane_low, pack_recv[first] - step, pack_recv[first + 1] + step)
+
+    near = jnp.where(sub == 0, step_x.astype(F32), 0.0)
+    for c in pack_copies[0:3]:
+        c.wait_recv()
+    early = jnp.concatenate([pair(0, 2), pack_recv[2] + near], axis=1)
+    col[256:512, :] = early.T
+    radial_rows(1)
+    both_early, hot_early = left_rows(early)
+    for q, s in enumerate(gather_sums(both_early, 1)):
+        sent[q] = sent[q] + s
+
+    for c in pack_copies[3:6]:
+        c.wait_recv()
+    late = jnp.concatenate([pack_recv[3] - near, pair(4, 1)], axis=1)
+    col[512:768, :] = late.T
+    radial_rows(2)
+    both_late, hot_late = left_rows(late)
+    sums = [sent[q] + s for q, s in enumerate(gather_sums(both_late, 2))]
+
+    agg = jnp.concatenate([s[0:8] for s in sums], axis=0)
+    a_high, a_low = split(agg)
+    chosen = dot(jnp.concatenate([a_high, a_low], axis=0).astype(BF16), sel[...])
+    chosen = chosen[0:32] + chosen[32:64]
+    for g in range(4):
+        agg_send[g] = chosen[:, g * 128 : (g + 1) * 128]
+    agg_copies = sends(agg_send, agg_recv, 6)
+    for n in (3, 4, 5, 0, 1, 2):
+        agg_copies[n].start()
+
+    loads[5].wait()
+    loads[6].wait()
     filt = filt_ref[...].astype(F32)
     emb = emb_ref[...].astype(F32)
     emb8 = jnp.concatenate([emb, emb], axis=0)
@@ -215,54 +252,16 @@
         axis=0,
     )
     w_high, w_low = split(first_w)
-    w_msg[...] = jnp.concatenate([w_high, w_high, w_low, jnp.zeros((32, WIDTH), F32)], axis=0).T.astype(BF16)
-    w_emb[...] = jnp.concatenate(
-        [jnp.zeros((96, WIDTH), F32), jnp.where(upper, emb8, 0.0), jnp.zeros((24, WIDTH), F32)], axis=0
-    ).T.astype(BF16)
-    filt_t = (SCALE * filt[1]).T
+    w_msg[...] = jnp.concatenate([w_high, w_high, w_low, jnp.where(upper, emb8, 0.0), SCALE * filt[1], jnp.zeros((16, WIDTH), F32)], axis=0).T.astype(BF16)
     for k in range(KB):
-        fbc[k] = jnp.broadcast_to(filt_t[:, k : k + 1], (WIDTH, 128)).astype(BF16)
-    loads[5].wait()
-    loads[6].wait()
+        ones = jnp.where(iota((128, 128), 0) == 104 + k, 1.0, 0.0).astype(BF16)
+        fbc[k] = dot(w_msg[...], ones).astype(BF16)
+    loads[7].wait()
+    loads[8].wait()
     for l in range(2):
         for m in range(MODELS):
             uvt[l, m, :, 0:128] = u_vm[l, m].astype(F32).T.astype(BF16)
             uvt[l, m, :, 128:256] = v_vm[l, m].astype(F32).T.astype(BF16)
-
-    lane_low = iota((8, 128), 1) < 64
-    sub = iota((8, 128), 0)
-
-    def pair(first, axis):
-        step = jnp.where(sub == axis, 1.0, 0.0)
-        return jnp.where(lane_low, pack_recv[first] - step, pack_recv[first + 1] + step)
-
-    near = jnp.where(sub == 0, step_x.astype(F32), 0.0)
-    for c in pack_copies[0:3]:
-        c.wait_recv()
-    early = jnp.concatenate([pair(0, 2), pack_recv[2] + near], axis=1)
-    col[256:512, :] = early.T
-    radial_rows(1)
-    both_early, hot_early = left_rows(early)
-    for q, s in enumerate(gather_sums(both_early, 1)):
-        sent[q] = sent[q] + s
-
-    for c in pack_copies[3:6]:
-        c.wait_recv()
-    late = jnp.concatenate([pack_recv[3] - near, pair(4, 1)], axis=1)
-    col[512:768, :] = late.T
-    radial_rows(2)
-    both_late, hot_late = left_rows(late)
-    sums = [sent[q] + s for q, s in enumerate(gather_sums(both_late, 2))]
-
-    agg = jnp.concatenate([s[0:8] for s in sums], axis=0)
-    a_high, a_low = split(agg)
-    chosen = dot(jnp.concatenate([a_high, a_low], axis=0).astype(BF16), sel[...])
-    chosen = chosen[0:32] + chosen[32:64]
-    for g in range(4):
-        agg_send[g] = chosen[:, g * 128 : (g + 1) * 128]
-    agg_copies = sends(agg_send, agg_recv, 6)
-    for n in (3, 4, 5, 0, 1, 2):
-        agg_copies[n].start()
 
     for q in range(4):
         for odd in range(2):
@@ -279,27 +278,30 @@
     def first_layer(table, hot):
         n = table.shape[1]
         t_high, t_low = split(table)
-        x = jnp.concatenate([t_high, t_low, t_high, hot, jnp.zeros((24, n), F32)], axis=0).astype(BF16)
+        blank = jnp.zeros((32, n), F32)
+        x = jnp.concatenate([t_high, t_low, t_high, blank], axis=0).astype(BF16)
+        z = jnp.concatenate([blank, blank, blank, hot, blank[0:24]], axis=0).astype(BF16)
         result = []
         for m in range(MODELS):
             rows = slice(m * C, (m + 1) * C)
             msg = dot(w_msg[rows, :], x).astype(BF16)
-            h = dot(w_emb[rows, :], x)
+            h = dot(w_msg[rows, :], z)
             pre = dot(uvt[0, m], jnp.concatenate([msg, h.astype(BF16)], axis=0))
             result.append(add_silu(h, pre))
         return result
 
-    def weigh(m, h):
+    def messages(m, h, part):
         rows = slice(m * C, (m + 1) * C)
+        tiles = []
         for k in range(KB):
             for half in range(2):
-                lanes = slice(half * 128, (half + 1) * 128)
-                h_tab[rows, k * 256 + half * 128 : k * 256 + (half + 1) * 128] = h[:, lanes] * fbc[k, rows, :]
+                tiles.append(h[:, half * 128 : (half + 1) * 128] * fbc[k, rows, :])
+        return dot(jnp.concatenate(tiles, axis=1), rad[part])
 
     for m, h in enumerate(first_layer(agg, hot_own)):
-        h_own[m * C : (m + 1) * C, :] = h
-        weigh(m, h.astype(BF16))
-    acc[...] = dot(h_tab[...], rad[0])
+        rows = slice(m * C, (m + 1) * C)
+        h_own[rows, :] = h
+        acc[rows, :] = messages(m, h.astype(BF16), 0)
 
     wide_low = iota((32, 128), 1) < 64
 
@@ -309,22 +311,24 @@
     for c in agg_copies[0:3]:
         c.wait_recv()
     for m, h in enumerate(first_layer(jnp.concatenate([agg_pair(0), agg_recv[2]], axis=1), hot_early)):
-        weigh(m, h.astype(BF16))
-    acc[...] += dot(h_tab[...], rad[1])
+        rows = slice(m * C, (m + 1) * C)
+        acc[rows, :] += messages(m, h.astype(BF16), 1)
     for c in agg_copies[3:6]:
         c.wait_recv()
+    message = []
     for m, h in enumerate(first_layer(jnp.concatenate([agg_recv[3], agg_pair(4)], axis=1), hot_late)):
-        weigh(m, h.astype(BF16))
-    message = (acc[...] + dot(h_tab[...], rad[2])).astype(BF16)
+        rows = slice(m * C, (m + 1) * C)
+        message.append((acc[rows, :] + messages(m, h.astype(BF16), 2)).astype(BF16))
 
     forces = []
+    loads[9].wait()
     for m in range(MODELS):
         rows = slice(m * C, (m + 1) * C)
-        x = jnp.concatenate([message[rows], h_own[rows, :].astype(BF16)], axis=0)
+        x = jnp.concatenate([message[m], h_own[rows, :].astype(BF16)], axis=0)
         h = add_silu(h_own[rows, :], dot(uvt[1, m], x))
         coeff = dot(fw_ref[m], h.astype(BF16))
         forces.append([SCALE * jnp.sum(coeff * dsum[c], axis=0, keepdims=True) for c in range(3)])
-    loads[7].wait()
+    loads[10].wait()
     alive = jnp.where(iota((1, ATOMS_DEV), 1) < live_ref[...], 1.0, 0.0)
     spread = jnp.zeros((1, ATOMS_DEV), F32)
     for c in range(3):
@@ -348,7 +352,7 @@
         mean, spread = pl.pallas_call(
             functools.partial(kernel, sizes),
             out_shape=(pltpu.VMEM((3, ATOMS_DEV), F32), pltpu.VMEM((1, ATOMS_DEV), F32)),
-            in_specs=[anywhere] * 6 + [vmem, vmem, anywhere, anywhere, vmem],
+            in_specs=[anywhere] * 11,
             out_specs=(vmem, vmem),
             scratch_shapes=[
                 pltpu.VMEM((3, ATOMS_DEV), F32),
@@ -359,6 +363,9 @@
                 pltpu.VMEM((4, 64), jnp.int32),
                 pltpu.VMEM((2, MODELS, C, C), BF16),
                 pltpu.VMEM((2, MODELS, C, C), BF16),
+                pltpu.VMEM((SPECIES, WIDTH), BF16),
+                pltpu.VMEM((2, KB, WIDTH), BF16),
+                pltpu.VMEM((MODELS, KB, C), BF16),
                 pltpu.VMEM((ATOMS_DEV, GHOSTS), BF16),
                 pltpu.VMEM((4, 8, 128), F32),
                 pltpu.VMEM((6, 8, 128), F32),
@@ -374,12 +381,11 @@
                 pltpu.VMEM((KB, WIDTH, 128), BF16),
                 pltpu.VMEM((2, MODELS, C, 2 * C), BF16),
                 pltpu.VMEM((WIDTH, 128), BF16),
-                pltpu.VMEM((WIDTH, 128), BF16),
                 pltpu.VMEM((3, KB, ATOMS_DEV), F32),
                 pltpu.VMEM((4, 32, ATOMS_DEV), F32),
                 pltpu.SemaphoreType.DMA((12,)),
                 pltpu.SemaphoreType.DMA((12,)),
-                pltpu.SemaphoreType.DMA((8,)),
+                pltpu.SemaphoreType.DMA((11,)),
             ],
             compiler_params=pltpu.CompilerParams(
                 collective_id=0, has_side_effects=True, vmem_limit_bytes=60 * 1024 * 1024

time: 23.8 us -> 21.4 us (0.90)
  the two profiles are of different devices: /device:TPU:2 before, /device:TPU:1 now
where the time goes in v3:
time: 21.4 us; the launch traced here: 21 us
  Pallas kernels  18.6 us (87%)
  between operations  1.29 us (6%)
  local copies, waits for them, and re-layouts  1.16 us (5%)
    pallas_call x1, Pallas kernels, local(): pl.pallas_call(functools.partial(kernel, sizes), out_shape=(pltpu.VMEM((3...  18.6 us
    unnamed x2, local copies, waits for them, and re-layouts  1.16 us

profile of v3, /device:TPU:1, one launch (start us, length us, event | category | flops | bytes accessed | tf_op | source)
XLA Modules:
  0.0 21.0 jit_solution(4576627167801507379)
XLA Ops:
  1.3 18.6 %shard_map.122 = (f32[3,256]{1,0:T(4,128)S(1)}, f32[1,256]{1,0:T(1,128)S(1)}) custom-call(f32[3,256]{1,0:T(4,128)} %pos_hbm.1, s32[1,256]{1,0:T(1,128)} %bitcast.10, s32[64,256]{1,0:T(8,128)} %nbr_hbm.1, s32[1,1]{1,0:T(1,128)} %bitcast.6.live_hbm, s32[2,128]{1,0:T(2,128)} %bitcast.11, s32[4,64]{1,0:T(4,128)} %bitcast.9, bf16[4,512]{1,0:T(4,128)(2,1)} %emb_hbm.1, ...), custom_call_target="tpu_custom_call" | custom-call | tf_op jit(solution)/shard_map/pallas_call | solution.py:352
  19.9 0.6 %copy.15 = f32[3,256]{1,0:T(4,128)} copy(f32[3,256]{1,0:T(4,128)S(1)} %get-tuple-element.6) | data formatting | bytes 6144
  20.5 0.6 %copy.16 = f32[256]{0:T(256)} copy(f32[256]{0:T(256)S(1)} %bitcast.7) | data formatting | bytes 2048

commit v4 on v3

--- a/solution.py
+++ b/solution.py
@@ -50,7 +50,7 @@
     pos_hbm, spec_hbm, nbr_hbm, live_hbm, gx_hbm, gyz_hbm, emb_hbm, filt_hbm, u_hbm, v_hbm, fw_hbm,
     mean_ref, dev_ref,
     pos_ref, spec_ref, nbr_ref, live_ref, gx_ref, gyz_ref, u_vm, v_vm, emb_ref, filt_ref, fw_ref,
-    sel, pack_send, pack_recv, agg_send, agg_recv, slots, count, col, rad, h_own, h_tab, acc,
+    sel, pack_send, pack_recv, agg_send, agg_recv, slots, count, col, rad_own, rad_pair, rad_z, rad_x, rad_y, h_own, h_tab, acc,
     fbc, uvt, w_msg, dsum, sent,
     send_sem, recv_sem, copy_sem,
 ):
@@ -153,10 +153,10 @@
 
     centre = own[0:3]
 
-    def radial_rows(part):
+    def radial_rows(target, begin, many):
         rows = 32
-        for tile in range(256 // rows):
-            first = part * 256 + tile * rows
+        for tile in range(many // rows):
+            first = begin + tile * rows
             squared = None
             for c in range(3):
                 gap = col[first : first + rows, c : c + 1] - pos_ref[c : c + 1, :]
@@ -168,7 +168,7 @@
             mid = jnp.exp2(-(off * off)) * count[first : first + rows, :].astype(F32)
 
             def put(k, value):
-                rad[part, k * 256 + tile * rows : k * 256 + (tile + 1) * rows, :] = value.astype(BF16)
+                target[k * many + tile * rows : k * many + (tile + 1) * rows, :] = value.astype(BF16)
 
             put(4, mid)
             value = mid
@@ -194,13 +194,14 @@
         odd = jnp.concatenate([hot_high, blank, place, blank], axis=0)
         return jnp.concatenate([even.astype(BF16), odd.astype(BF16)], axis=1), hot
 
-    def gather_sums(both, part):
-        return [dot(both, rad[part, q * 512 : (q + 1) * 512, :]) for q in range(4)]
+    def gather_sums(both, target):
+        wide = target.shape[0] // 4
+        return [dot(both, target[q * wide : (q + 1) * wide, :]) for q in range(4)]
 
     col[0:256, :] = own.T
-    radial_rows(0)
+    radial_rows(rad_own, 0, 256)
     both_own, hot_own = left_rows(own)
-    for q, s in enumerate(gather_sums(both_own, 0)):
+    for q, s in enumerate(gather_sums(both_own, rad_own)):
         sent[q] = s
 
     lane_low = iota((8, 128), 1) < 64
@@ -211,22 +212,39 @@
         return jnp.where(lane_low, pack_recv[first] - step, pack_recv[first + 1] + step)
 
     near = jnp.where(sub == 0, step_x.astype(F32), 0.0)
-    for c in pack_copies[0:3]:
-        c.wait_recv()
-    early = jnp.concatenate([pair(0, 2), pack_recv[2] + near], axis=1)
-    col[256:512, :] = early.T
-    radial_rows(1)
-    both_early, hot_early = left_rows(early)
-    for q, s in enumerate(gather_sums(both_early, 1)):
-        sent[q] = sent[q] + s
-
-    for c in pack_copies[3:6]:
-        c.wait_recv()
-    late = jnp.concatenate([pack_recv[3] - near, pair(4, 1)], axis=1)
-    col[512:768, :] = late.T
-    radial_rows(2)
-    both_late, hot_late = left_rows(late)
-    sums = [sent[q] + s for q, s in enumerate(gather_sums(both_late, 2))]
+    lent_hot = {}
+    sums = [sent[q] for q in range(4)]
+    for c in pack_copies[slice(2, 3)]:
+        c.wait_recv()
+    lent = pack_recv[2] + near
+    col[384:512, :] = lent.T
+    radial_rows(rad_pair, 384, 128)
+    both_lent, lent_hot["p"] = left_rows(lent)
+    sums = [a + b for a, b in zip(sums, gather_sums(both_lent, rad_pair))]
+
+    for c in pack_copies[slice(0, 2)]:
+        c.wait_recv()
+    lent = pair(0, 2)
+    col[256:384, :] = lent.T
+    radial_rows(rad_z, 256, 128)
+    both_lent, lent_hot["z"] = left_rows(lent)
+    sums = [a + b for a, b in zip(sums, gather_sums(both_lent, rad_z))]
+
+    for c in pack_copies[slice(3, 4)]:
+        c.wait_recv()
+    lent = pack_recv[3] - near
+    col[512:640, :] = lent.T
+    radial_rows(rad_x, 512, 128)
+    both_lent, lent_hot["x"] = left_rows(lent)
+    sums = [a + b for a, b in zip(sums, gather_sums(both_lent, rad_x))]
+
+    for c in pack_copies[slice(4, 6)]:
+        c.wait_recv()
+    lent = pair(4, 1)
+    col[640:768, :] = lent.T
+    radial_rows(rad_y, 640, 128)
+    both_lent, lent_hot["y"] = left_rows(lent)
+    sums = [a + b for a, b in zip(sums, gather_sums(both_lent, rad_y))]
 
     agg = jnp.concatenate([s[0:8] for s in sums], axis=0)
     a_high, a_low = split(agg)
@@ -294,31 +312,41 @@
         rows = slice(m * C, (m + 1) * C)
         tiles = []
         for k in range(KB):
-            for half in range(2):
+            for half in range(h.shape[1] // 128):
                 tiles.append(h[:, half * 128 : (half + 1) * 128] * fbc[k, rows, :])
-        return dot(jnp.concatenate(tiles, axis=1), rad[part])
+        return dot(jnp.concatenate(tiles, axis=1), part[...])
 
     for m, h in enumerate(first_layer(agg, hot_own)):
         rows = slice(m * C, (m + 1) * C)
         h_own[rows, :] = h
-        acc[rows, :] = messages(m, h.astype(BF16), 0)
+        acc[rows, :] = messages(m, h.astype(BF16), rad_own)
 
     wide_low = iota((32, 128), 1) < 64
 
     def agg_pair(first):
         return jnp.where(wide_low, agg_recv[first], agg_recv[first + 1])
 
-    for c in agg_copies[0:3]:
-        c.wait_recv()
-    for m, h in enumerate(first_layer(jnp.concatenate([agg_pair(0), agg_recv[2]], axis=1), hot_early)):
-        rows = slice(m * C, (m + 1) * C)
-        acc[rows, :] += messages(m, h.astype(BF16), 1)
-    for c in agg_copies[3:6]:
+    for c in agg_copies[slice(2, 3)]:
+        c.wait_recv()
+    for m, h in enumerate(first_layer(agg_recv[2], lent_hot["p"])):
+        rows = slice(m * C, (m + 1) * C)
+        acc[rows, :] += messages(m, h.astype(BF16), rad_pair)
+    for c in agg_copies[slice(0, 2)]:
+        c.wait_recv()
+    for m, h in enumerate(first_layer(agg_pair(0), lent_hot["z"])):
+        rows = slice(m * C, (m + 1) * C)
+        acc[rows, :] += messages(m, h.astype(BF16), rad_z)
+    for c in agg_copies[slice(3, 4)]:
+        c.wait_recv()
+    for m, h in enumerate(first_layer(agg_recv[3], lent_hot["x"])):
+        rows = slice(m * C, (m + 1) * C)
+        acc[rows, :] += messages(m, h.astype(BF16), rad_x)
+    for c in agg_copies[slice(4, 6)]:
         c.wait_recv()
     message = []
-    for m, h in enumerate(first_layer(jnp.concatenate([agg_recv[3], agg_pair(4)], axis=1), hot_late)):
-        rows = slice(m * C, (m + 1) * C)
-        message.append((acc[rows, :] + messages(m, h.astype(BF16), 2)).astype(BF16))
+    for m, h in enumerate(first_layer(agg_pair(4), lent_hot["y"])):
+        rows = slice(m * C, (m + 1) * C)
+        message.append((acc[rows, :] + messages(m, h.astype(BF16), rad_y)).astype(BF16))
 
     forces = []
     loads[9].wait()
@@ -374,7 +402,11 @@
                 pltpu.VMEM((3 * SLOTS_HALF, 16, ATOMS_DEV), BF16),
                 pltpu.VMEM((TABLE, ATOMS_DEV), BF16),
                 pltpu.VMEM((TABLE, 8), F32),
-                pltpu.VMEM((3, KB * 256, ATOMS_DEV), BF16),
+                pltpu.VMEM((KB * 256, ATOMS_DEV), BF16),
+                pltpu.VMEM((KB * 128, ATOMS_DEV), BF16),
+                pltpu.VMEM((KB * 128, ATOMS_DEV), BF16),
+                pltpu.VMEM((KB * 128, ATOMS_DEV), BF16),
+                pltpu.VMEM((KB * 128, ATOMS_DEV), BF16),
                 pltpu.VMEM((WIDTH, ATOMS_DEV), F32),
                 pltpu.VMEM((WIDTH, KB * 256), BF16),
                 pltpu.VMEM((WIDTH, ATOMS_DEV), F32),

time: 21.4 us -> 20.8 us (0.972); the launches traced: 21 us -> 20.7 us
  Pallas kernels: 18.6 us -> 18.3 us
    pallas_call x1, Pallas kernels: 18.6 us -> 18.3 us  [local(): pl.pallas_call(functools.partial(kernel, sizes), out_shape=(pltpu.VMEM((3...]
where the time goes in v4:
time: 20.8 us; the launch traced here: 20.7 us
  Pallas kernels  18.3 us (88%)
  between operations  1.29 us (6%)
  local copies, waits for them, and re-layouts  1.16 us (6%)
    pallas_call x1, Pallas kernels, local(): pl.pallas_call(functools.partial(kernel, sizes), out_shape=(pltpu.VMEM((3...  18.3 us
    unnamed x2, local copies, waits for them, and re-layouts  1.16 us

profile of v4, /device:TPU:1, one launch (start us, length us, event | category | flops | bytes accessed | tf_op | source)
XLA Modules:
  0.0 20.7 jit_solution(2588413809629096782)
XLA Ops:
  1.3 18.3 %shard_map.122 = (f32[3,256]{1,0:T(4,128)S(1)}, f32[1,256]{1,0:T(1,128)S(1)}) custom-call(f32[3,256]{1,0:T(4,128)} %pos_hbm.1, s32[1,256]{1,0:T(1,128)} %bitcast.10, s32[64,256]{1,0:T(8,128)} %nbr_hbm.1, s32[1,1]{1,0:T(1,128)} %bitcast.6.live_hbm, s32[2,128]{1,0:T(2,128)} %bitcast.11, s32[4,64]{1,0:T(4,128)} %bitcast.9, bf16[4,512]{1,0:T(4,128)(2,1)} %emb_hbm.1, ...), custom_call_target="tpu_custom_call" | custom-call | tf_op jit(solution)/shard_map/pallas_call | solution.py:380
  19.6 0.6 %copy.15 = f32[3,256]{1,0:T(4,128)} copy(f32[3,256]{1,0:T(4,128)S(1)} %get-tuple-element.6) | data formatting | bytes 6144
  20.1 0.6 %copy.16 = f32[256]{0:T(256)} copy(f32[256]{0:T(256)S(1)} %bitcast.7) | data formatting | bytes 2048

commit v5 on v4

--- a/solution.py
+++ b/solution.py
@@ -203,58 +203,6 @@
     both_own, hot_own = left_rows(own)
     for q, s in enumerate(gather_sums(both_own, rad_own)):
         sent[q] = s
-
-    lane_low = iota((8, 128), 1) < 64
-    sub = iota((8, 128), 0)
-
-    def pair(first, axis):
-        step = jnp.where(sub == axis, 1.0, 0.0)
-        return jnp.where(lane_low, pack_recv[first] - step, pack_recv[first + 1] + step)
-
-    near = jnp.where(sub == 0, step_x.astype(F32), 0.0)
-    lent_hot = {}
-    sums = [sent[q] for q in range(4)]
-    for c in pack_copies[slice(2, 3)]:
-        c.wait_recv()
-    lent = pack_recv[2] + near
-    col[384:512, :] = lent.T
-    radial_rows(rad_pair, 384, 128)
-    both_lent, lent_hot["p"] = left_rows(lent)
-    sums = [a + b for a, b in zip(sums, gather_sums(both_lent, rad_pair))]
-
-    for c in pack_copies[slice(0, 2)]:
-        c.wait_recv()
-    lent = pair(0, 2)
-    col[256:384, :] = lent.T
-    radial_rows(rad_z, 256, 128)
-    both_lent, lent_hot["z"] = left_rows(lent)
-    sums = [a + b for a, b in zip(sums, gather_sums(both_lent, rad_z))]
-
-    for c in pack_copies[slice(3, 4)]:
-        c.wait_recv()
-    lent = pack_recv[3] - near
-    col[512:640, :] = lent.T
-    radial_rows(rad_x, 512, 128)
-    both_lent, lent_hot["x"] = left_rows(lent)
-    sums = [a + b for a, b in zip(sums, gather_sums(both_lent, rad_x))]
-
-    for c in pack_copies[slice(4, 6)]:
-        c.wait_recv()
-    lent = pair(4, 1)
-    col[640:768, :] = lent.T
-    radial_rows(rad_y, 640, 128)
-    both_lent, lent_hot["y"] = left_rows(lent)
-    sums = [a + b for a, b in zip(sums, gather_sums(both_lent, rad_y))]
-
-    agg = jnp.concatenate([s[0:8] for s in sums], axis=0)
-    a_high, a_low = split(agg)
-    chosen = dot(jnp.concatenate([a_high, a_low], axis=0).astype(BF16), sel[...])
-    chosen = chosen[0:32] + chosen[32:64]
-    for g in range(4):
-        agg_send[g] = chosen[:, g * 128 : (g + 1) * 128]
-    agg_copies = sends(agg_send, agg_recv, 6)
-    for n in (3, 4, 5, 0, 1, 2):
-        agg_copies[n].start()
 
     loads[5].wait()
     loads[6].wait()
@@ -274,6 +222,58 @@
     for k in range(KB):
         ones = jnp.where(iota((128, 128), 0) == 104 + k, 1.0, 0.0).astype(BF16)
         fbc[k] = dot(w_msg[...], ones).astype(BF16)
+    lane_low = iota((8, 128), 1) < 64
+    sub = iota((8, 128), 0)
+
+    def pair(first, axis):
+        step = jnp.where(sub == axis, 1.0, 0.0)
+        return jnp.where(lane_low, pack_recv[first] - step, pack_recv[first + 1] + step)
+
+    near = jnp.where(sub == 0, step_x.astype(F32), 0.0)
+    lent_hot = {}
+    sums = [sent[q] for q in range(4)]
+    for c in pack_copies[slice(2, 3)]:
+        c.wait_recv()
+    lent = pack_recv[2] + near
+    col[384:512, :] = lent.T
+    radial_rows(rad_pair, 384, 128)
+    both_lent, lent_hot["p"] = left_rows(lent)
+    sums = [a + b for a, b in zip(sums, gather_sums(both_lent, rad_pair))]
+
+    for c in pack_copies[slice(0, 2)]:
+        c.wait_recv()
+    lent = pair(0, 2)
+    col[256:384, :] = lent.T
+    radial_rows(rad_z, 256, 128)
+    both_lent, lent_hot["z"] = left_rows(lent)
+    sums = [a + b for a, b in zip(sums, gather_sums(both_lent, rad_z))]
+
+    for c in pack_copies[slice(3, 4)]:
+        c.wait_recv()
+    lent = pack_recv[3] - near
+    col[512:640, :] = lent.T
+    radial_rows(rad_x, 512, 128)
+    both_lent, lent_hot["x"] = left_rows(lent)
+    sums = [a + b for a, b in zip(sums, gather_sums(both_lent, rad_x))]
+
+    for c in pack_copies[slice(4, 6)]:
+        c.wait_recv()
+    lent = pair(4, 1)
+    col[640:768, :] = lent.T
+    radial_rows(rad_y, 640, 128)
+    both_lent, lent_hot["y"] = left_rows(lent)
+    sums = [a + b for a, b in zip(sums, gather_sums(both_lent, rad_y))]
+
+    agg = jnp.concatenate([s[0:8] for s in sums], axis=0)
+    a_high, a_low = split(agg)
+    chosen = dot(jnp.concatenate([a_high, a_low], axis=0).astype(BF16), sel[...])
+    chosen = chosen[0:32] + chosen[32:64]
+    for g in range(4):
+        agg_send[g] = chosen[:, g * 128 : (g + 1) * 128]
+    agg_copies = sends(agg_send, agg_recv, 6)
+    for n in (3, 4, 5, 0, 1, 2):
+        agg_copies[n].start()
+
     loads[7].wait()
     loads[8].wait()
     for l in range(2):
@@ -357,7 +357,7 @@
         coeff = dot(fw_ref[m], h.astype(BF16))
         forces.append([SCALE * jnp.sum(coeff * dsum[c], axis=0, keepdims=True) for c in range(3)])
     loads[10].wait()
-    alive = jnp.where(iota((1, ATOMS_DEV), 1) < live_ref[...], 1.0, 0.0)
+    alive = jnp.where(iota((1, ATOMS_DEV), 1) < live_ref[0], 1.0, 0.0)
     spread = jnp.zeros((1, ATOMS_DEV), F32)
     for c in range(3):
         mean = (forces[0][c] + forces[1][c] + forces[2][c] + forces[3][c]) * 0.25
@@ -386,7 +386,7 @@
                 pltpu.VMEM((3, ATOMS_DEV), F32),
                 pltpu.VMEM((1, ATOMS_DEV), jnp.int32),
                 pltpu.VMEM((2 * SLOTS_HALF, ATOMS_DEV), jnp.int32),
-                pltpu.VMEM((1, 1), jnp.int32),
+                pltpu.SMEM((1,), jnp.int32),
                 pltpu.VMEM((2, 128), jnp.int32),
                 pltpu.VMEM((4, 64), jnp.int32),
                 pltpu.VMEM((2, MODELS, C, C), BF16),
@@ -426,7 +426,7 @@
             positions,
             species.reshape(1, ATOMS_DEV),
             neighbors,
-            atom_count.reshape(1, 1),
+            atom_count,
             ghost_x.reshape(2, 2 * 64),
             ghost_yz.reshape(4, 64),
             embedding,

time: 20.8 us -> 20.8 us (level)
  no operation moved by 1% of the time
where the time goes in v5:
time: 20.8 us; the launch traced here: 20.7 us
  Pallas kernels  18.2 us (88%)
  between operations  1.29 us (6%)
  local copies, waits for them, and re-layouts  1.16 us (6%)
    pallas_call x1, Pallas kernels, local(): pl.pallas_call(functools.partial(kernel, sizes), out_shape=(pltpu.VMEM((3...  18.2 us
    unnamed x2, local copies, waits for them, and re-layouts  1.16 us

profile of v5, /device:TPU:1, one launch (start us, length us, event | category | flops | bytes accessed | tf_op | source)
XLA Modules:
  0.0 20.7 jit_solution(3051035490379443503)
XLA Ops:
  1.3 18.2 %shard_map.122 = (f32[3,256]{1,0:T(4,128)S(1)}, f32[1,256]{1,0:T(1,128)S(1)}) custom-call(f32[3,256]{1,0:T(4,128)} %pos_hbm.1, s32[1,256]{1,0:T(1,128)} %bitcast.8, s32[64,256]{1,0:T(8,128)} %nbr_hbm.1, s32[1]{0:T(128)S(6)} %copy.17.live_hbm, s32[2,128]{1,0:T(2,128)} %bitcast.9, s32[4,64]{1,0:T(4,128)} %bitcast.7, bf16[4,512]{1,0:T(4,128)(2,1)} %emb_hbm.1, ...), custom_call_target="tpu_custom_call" | custom-call | tf_op jit(solution)/shard_map/pallas_call | solution.py:380
  19.5 0.6 %copy.15 = f32[3,256]{1,0:T(4,128)} copy(f32[3,256]{1,0:T(4,128)S(1)} %get-tuple-element.6) | data formatting | bytes 6144
  20.1 0.6 %copy.16 = f32[256]{0:T(256)} copy(f32[256]{0:T(256)S(1)} %bitcast.5) | data formatting | bytes 2048

commit v6 on v5

--- a/solution.py
+++ b/solution.py
@@ -47,9 +47,9 @@
 
 def kernel(
     sizes,
-    pos_hbm, spec_hbm, nbr_hbm, live_hbm, gx_hbm, gyz_hbm, emb_hbm, filt_hbm, u_hbm, v_hbm, fw_hbm,
+    pos_hbm, spec_hbm, nbr_hbm, live_hbm, gx_hbm, gyz_hbm, emb_ref, filt_ref, u_hbm, v_hbm, fw_ref,
     mean_ref, dev_ref,
-    pos_ref, spec_ref, nbr_ref, live_ref, gx_ref, gyz_ref, u_vm, v_vm, emb_ref, filt_ref, fw_ref,
+    pos_ref, spec_ref, nbr_ref, live_ref, gx_ref, gyz_ref, u_vm, v_vm,
     sel, pack_send, pack_recv, agg_send, agg_recv, slots, count, col, rad_own, rad_pair, rad_z, rad_x, rad_y, h_own, h_tab, acc,
     fbc, uvt, w_msg, dsum, sent,
     send_sem, recv_sem, copy_sem,
@@ -71,7 +71,7 @@
         for n, (source, target) in enumerate(
             (
                 (gx_hbm, gx_ref), (gyz_hbm, gyz_ref), (pos_hbm, pos_ref), (spec_hbm, spec_ref),
-                (nbr_hbm, nbr_ref), (emb_hbm, emb_ref), (filt_hbm, filt_ref), (u_hbm, u_vm), (v_hbm, v_vm), (fw_hbm, fw_ref), (live_hbm, live_ref),
+                (nbr_hbm, nbr_ref), (u_hbm, u_vm), (v_hbm, v_vm), (live_hbm, live_ref),
             )
         )
     ]
@@ -204,8 +204,6 @@
     for q, s in enumerate(gather_sums(both_own, rad_own)):
         sent[q] = s
 
-    loads[5].wait()
-    loads[6].wait()
     filt = filt_ref[...].astype(F32)
     emb = emb_ref[...].astype(F32)
     emb8 = jnp.concatenate([emb, emb], axis=0)
@@ -274,8 +272,8 @@
     for n in (3, 4, 5, 0, 1, 2):
         agg_copies[n].start()
 
-    loads[7].wait()
-    loads[8].wait()
+    loads[5].wait()
+    loads[6].wait()
     for l in range(2):
         for m in range(MODELS):
             uvt[l, m, :, 0:128] = u_vm[l, m].astype(F32).T.astype(BF16)
@@ -349,14 +347,13 @@
         message.append((acc[rows, :] + messages(m, h.astype(BF16), rad_y)).astype(BF16))
 
     forces = []
-    loads[9].wait()
     for m in range(MODELS):
         rows = slice(m * C, (m + 1) * C)
         x = jnp.concatenate([message[m], h_own[rows, :].astype(BF16)], axis=0)
         h = add_silu(h_own[rows, :], dot(uvt[1, m], x))
         coeff = dot(fw_ref[m], h.astype(BF16))
         forces.append([SCALE * jnp.sum(coeff * dsum[c], axis=0, keepdims=True) for c in range(3)])
-    loads[10].wait()
+    loads[7].wait()
     alive = jnp.where(iota((1, ATOMS_DEV), 1) < live_ref[0], 1.0, 0.0)
     spread = jnp.zeros((1, ATOMS_DEV), F32)
     for c in range(3):
@@ -380,7 +377,7 @@
         mean, spread = pl.pallas_call(
             functools.partial(kernel, sizes),
             out_shape=(pltpu.VMEM((3, ATOMS_DEV), F32), pltpu.VMEM((1, ATOMS_DEV), F32)),
-            in_specs=[anywhere] * 11,
+            in_specs=[anywhere] * 6 + [vmem, vmem, anywhere, anywhere, vmem],
             out_specs=(vmem, vmem),
             scratch_shapes=[
                 pltpu.VMEM((3, ATOMS_DEV), F32),
@@ -391,9 +388,6 @@
                 pltpu.VMEM((4, 64), jnp.int32),
                 pltpu.VMEM((2, MODELS, C, C), BF16),
                 pltpu.VMEM((2, MODELS, C, C), BF16),
-                pltpu.VMEM((SPECIES, WIDTH), BF16),
-                pltpu.VMEM((2, KB, WIDTH), BF16),
-                pltpu.VMEM((MODELS, KB, C), BF16),
                 pltpu.VMEM((ATOMS_DEV, GHOSTS), BF16),
                 pltpu.VMEM((4, 8, 128), F32),
                 pltpu.VMEM((6, 8, 128), F32),
@@ -417,7 +411,7 @@
                 pltpu.VMEM((4, 32, ATOMS_DEV), F32),
                 pltpu.SemaphoreType.DMA((12,)),
                 pltpu.SemaphoreType.DMA((12,)),
-                pltpu.SemaphoreType.DMA((11,)),
+                pltpu.SemaphoreType.DMA((8,)),
             ],
             compiler_params=pltpu.CompilerParams(
                 collective_id=0, has_side_effects=True, vmem_limit_bytes=60 * 1024 * 1024

time: 20.8 us -> 21.4 us (1.029)
  Pallas kernels: 18.2 us -> 18.7 us
    pallas_call x1, Pallas kernels: 18.2 us -> 18.7 us  [local(): pl.pallas_call(functools.partial(kernel, sizes), out_shape=(pltpu.VMEM((3...]
where the time goes in v6:
time: 21.4 us; the launch traced here: 21.1 us
  Pallas kernels  18.7 us (87%)
  between operations  1.29 us (6%)
  local copies, waits for them, and re-layouts  1.16 us (5%)
    pallas_call x1, Pallas kernels, local(): pl.pallas_call(functools.partial(kernel, sizes), out_shape=(pltpu.VMEM((3...  18.7 us
    unnamed x2, local copies, waits for them, and re-layouts  1.16 us

profile of v6, /device:TPU:1, one launch (start us, length us, event | category | flops | bytes accessed | tf_op | source)
XLA Modules:
  0.0 21.1 jit_solution(15875459776039950837)
XLA Ops:
  1.3 18.7 %shard_map.122 = (f32[3,256]{1,0:T(4,128)S(1)}, f32[1,256]{1,0:T(1,128)S(1)}) custom-call(f32[3,256]{1,0:T(4,128)} %pos_hbm.1, s32[1,256]{1,0:T(1,128)} %bitcast.8, s32[64,256]{1,0:T(8,128)} %nbr_hbm.1, s32[1]{0:T(128)S(6)} %copy.17.live_hbm, s32[2,128]{1,0:T(2,128)} %bitcast.9, s32[4,64]{1,0:T(4,128)} %bitcast.7, bf16[4,512]{1,0:T(4,128)(2,1)} %emb_ref.1, ...), custom_call_target="tpu_custom_call" | custom-call | tf_op jit(solution)/shard_map/pallas_call | solution.py:377
  20.0 0.6 %copy.15 = f32[3,256]{1,0:T(4,128)} copy(f32[3,256]{1,0:T(4,128)S(1)} %get-tuple-element.6) | data formatting | bytes 6144
  20.6 0.6 %copy.16 = f32[256]{0:T(256)} copy(f32[256]{0:T(256)S(1)} %bitcast.5) | data formatting | bytes 2048
